TPU v7x, 512 devices: a whole 4x8x8 slice. The times are simulated.
512 devices in a mesh: context: 32 (over z_hi, y, core), tensor: 16 (over z_lo, x).
Axes of the slice: x: 4, y: 8, z: 8 (z_hi: 2, z_lo: 4; z = z_hi * 4 + z_lo), core: 2. Of those that a mesh axis runs over, the one named last changes fastest.
Arguments:
- queries: bfloat16 [8192, 16384], P('context', 'tensor')
- key_value_rows: bfloat16 [2, 8192, 1024], P(None, ('context', 'tensor'))
- positions: int32 [8192], P('context'), may hold values from 0 to 8191, as said below
Outputs:
- attended: bfloat16 [8192, 16384], P(('context', 'tensor'))
Inputs may be any that keep to these rules, and one draw needn't show every extreme that they name: positions is a permutation of 0 .. 8191 made of 64 blocks of 128 consecutive rising positions; each aligned run of 256 tokens holds block j and block 63 - j for some j, in either order.
All inputs are finite; a program needn't handle non-finite values.
Results may differ from a plain program's by a relative error of at most 0.007.
Values may be sent and summed in bfloat16 or wider, within the bound.
A program may use at most 64 MiB of HBM per device.

v0:
```python
import math

import jax
import jax.numpy as jnp
from jax import lax
from jax.sharding import PartitionSpec as P

HEAD_SIZE = 128


NEGATIVE = -1e30


def frequencies(width):
    counter = jnp.arange(width // 2, dtype=jnp.float32)
    inverse = 500000.0 ** (-2.0 * counter / width)
    wavelength = 2.0 * math.pi / inverse
    smooth = jnp.clip((8192.0 / wavelength - 1.0) / 3.0, 0.0, 1.0)
    return (1.0 - smooth) * inverse / 8.0 + smooth * inverse


def apply_rotary(value_matrix, places):
    width = value_matrix.shape[-1]
    half_width = width // 2
    angles = places.astype(jnp.float32)[:, None] * frequencies(width)[None, :]
    angles = angles.reshape(
        (value_matrix.shape[0],) + (1,) * (value_matrix.ndim - 2) + (half_width,)
    )
    cosine = jnp.cos(angles)
    sine = jnp.sin(angles)
    first = value_matrix[..., :half_width].astype(jnp.float32)
    second = value_matrix[..., half_width:].astype(jnp.float32)
    return jnp.concatenate(
        [first * cosine - second * sine, second * cosine + first * sine], axis=-1
    )


def local(queries, key_value_rows, positions):
    token_rows = queries.shape[0]
    width = HEAD_SIZE
    head_count = queries.shape[1] // width
    query_rows = token_rows * head_count
    scale = 1.0 / math.sqrt(width)
    rotated_q = apply_rotary(queries.reshape(token_rows, head_count, width), positions).astype(
        jnp.bfloat16
    )
    rotated_q = rotated_q.reshape(query_rows, width)
    query_places = jnp.repeat(positions, head_count)
    tensor_rank = lax.axis_index("tensor")
    whole = lax.all_gather(key_value_rows, "tensor", axis=1, tiled=True)
    head_start = tensor_rank // 2 * width
    mine = lax.dynamic_slice_in_dim(whole, head_start, width, 2)
    key_rows = mine[0]
    value_rows = mine[1]

    def attend(carry, key_block, value_block, place_block):
        running_max, running_sum, running_out = carry
        scores = jnp.dot(rotated_q, key_block.T, preferred_element_type=jnp.float32) * scale
        visible = place_block[None, :] <= query_places[:, None]
        scores = jnp.where(visible, scores, NEGATIVE)
        new_max = jnp.maximum(running_max, jnp.max(scores, axis=1))
        weights = jnp.where(visible, jnp.exp(scores - new_max[:, None]), 0.0)
        factor = jnp.exp(running_max - new_max)
        new_sum = running_sum * factor + jnp.sum(weights, axis=1)
        product = jnp.dot(
            weights.astype(jnp.bfloat16), value_block, preferred_element_type=jnp.float32
        )
        new_out = running_out * factor[:, None] + product
        return (new_max, new_sum, new_out)

    initial = (
        jnp.full((query_rows,), NEGATIVE, jnp.float32),
        jnp.zeros((query_rows,), jnp.float32),
        jnp.zeros((query_rows, width), jnp.float32),
    )
    carry = initial
    key_piece = lax.all_gather(key_rows, "context", axis=0, tiled=True)
    value_piece = lax.all_gather(value_rows, "context", axis=0, tiled=True)
    place_piece = lax.all_gather(positions, "context", axis=0, tiled=True)
    key_piece = apply_rotary(key_piece, place_piece).astype(jnp.bfloat16)
    count = key_piece.shape[0]
    block_rows = math.gcd(count, 1024)
    stacked = (
        key_piece.reshape(count // block_rows, block_rows, width),
        value_piece.reshape(count // block_rows, block_rows, width),
        place_piece.reshape(count // block_rows, block_rows),
    )

    def advance(state, block):
        key_block, value_block, place_block = block
        state = attend(state, key_block, value_block, place_block)
        return (state, None)

    carry, unused = lax.scan(advance, carry, stacked)
    final_max, final_sum, final_out = carry
    heads = (final_out / final_sum[:, None]).astype(jnp.bfloat16)
    heads = heads.reshape(token_rows, head_count * width)
    return lax.all_to_all(heads, "tensor", split_axis=0, concat_axis=1, tiled=True)


def solution(mesh):
    placed = (P("context", "tensor"), P(None, ("context", "tensor"), None), P("context"))
    return jax.shard_map(
        local, mesh=mesh, in_specs=placed, out_specs=P(("context", "tensor"), None), check_vma=False
    )
```

profile of v0, /device:TPU:6, one launch (start us, length us, event | category | flops | bytes accessed | tf_op | source)
XLA Modules:
  0.0 432.0 jit_solution(719821705230161708)
XLA Ops:
  6.5 0.7 all-gather.7.cloned.1.call-update
  7.3 86.2 %all-gather.7.cloned.1.call-done = bf16[2,256,1024]{2,1,0:T(8,128)(2,1)} async-done(((bf16[2,16,1024]{2,1,0:T(8,128)(2,1)}), bf16[2,256,1024]{2,1,0:T(8,128)(2,1)}) %all-gather.7.cloned.1.call-update) | async-done | bytes 1048592 | tf_op jit(solution)/shard_map/all_gather | solution.py:50
  93.5 1.5 constant_dynamic-slice_fusion.2
  95.1 0.7 all-gather.11.cloned.1.call-update
  95.8 0.7 convert_element_type.32
  96.5 1.1 copy.8
  97.6 52.0 %all-gather.2 = s32[32,1,256]{2,1,0:T(1,128)S(1)} all-gather(s32[1,1,256]{2,1,0:T(1,128)} %bitcast.62), channel_id=1, replica_groups=mesh['context'=32,'tensor'=16] {'context'}, dimensions={0}, use_global_device_ids=true | all-gather | bytes 33792 | tf_op jit(solution)/shard_map/all_gather | solution.py:79
  149.8 0.5 multiply_cosine_fusion.1
  150.3 0.5 fusion.34
  150.8 1.1 pad_maximum_fusion.1
  151.8 42.0 %all-gather.9.cloned.1.call-done = bf16[1,8192,128]{2,1,0:T(8,128)(2,1)} async-done(((bf16[1,256,128]{2,1,0:T(8,128)(2,1)}), bf16[1,8192,128]{2,1,0:T(8,128)(2,1)}) %all-gather.9.cloned.1.call-update) | async-done | bytes 2097168 | tf_op jit(solution)/shard_map/all_gather | solution.py:77
  193.9 19.4 %fusion.26 = (bf16[8192,64]{1,0:T(8,128)(2,1)S(1)}, bf16[8192,64]{1,0:T(8,128)(2,1)S(1)}) fusion(f32[64]{0:T(128)S(1)} %multiply_add_fusion, f32[8192]{0:T(1024)S(1)} %bitcast.61, bf16[8192,128]{1,0:T(8,128)(2,1)} %bitcast.52), kind=kLoop, calls=%fused_computation.31 | loop fusion | flops 5767168 | bytes 4227328 | tf_op jit(solution)/shard_map/convert.7
  213.3 1.2 pad_maximum_fusion
  214.5 70.6 %all-gather.11.cloned.1.call-done = bf16[1,8192,128]{2,1,0:T(8,128)(2,1)} async-done(((bf16[1,256,128]{2,1,0:T(8,128)(2,1)}), bf16[1,8192,128]{2,1,0:T(8,128)(2,1)}) %all-gather.11.cloned.1.call-update) | async-done | bytes 2097168 | tf_op jit(solution)/shard_map/all_gather | solution.py:78
  285.1 120.0 %while.15 = (s32[]{:T(128)}, f32[2048]{0:T(1024)S(1)}, f32[2048]{0:T(1024)S(1)}, f32[2048,128]{1,0:T(8,128)S(1)}, s32[8,1024]{1,0:T(8,128)S(1)}, /*index=5*/bf16...) while((s32[]{:T(128)}, f32[2048]{0:T(1024)S(1)}, ...), condition=%wide.region_3.4_spmd.clone, body=%wide.region_0.3_spmd.clone.sunk | while | flops 1108092928 | bytes 62068380 | solution.py:94
  285.1 0.1 broadcast_in_dim.59
  285.2 0.1 le.66
  285.3 5.0 %fusion.47 = (f32[2048]{0:T(1024)S(1)}, f32[1024,2048]{1,0:T(8,128)}) fusion(s32[2048]{0:T(1024)S(1)} %le.66, s32[1024]{0:T(1024)S(1)} %bitcast.58, bf16[2048,128]{1,0:T(8,128)(2,1)} %get-tuple-element.211, bf16[8,1024,128]{2,1,0:T(8,128)(2,1)S(1)} %get-tuple-element.210, s32[]{:T(128)} %get-tuple-element.194), kind=kOutput, calls=%fused_computation.3.clone.1 | convolution fusion | flops 545257472 | bytes 9195524 | tf_op jit(solution)/shard_map/while/body/eval_jaxpr/dot_general | solution.py:58
  290.3 5.5 %fusion.48 = f32[2048]{0:T(1024)S(1)} fusion(f32[1024,2048]{1,0:T(8,128)} %get-tuple-element.180, f32[2048]{0:T(1024)S(1)} %select_maximum_fusion.2, s32[2048]{0:T(1024)S(1)} %le.66, s32[1024]{0:T(1024)S(1)} %bitcast.59), kind=kLoop, calls=%fused_computation.5.clone.1 | loop fusion | flops 12580864 | bytes 8417280 | tf_op jit(solution)/shard_map/while/body/eval_jaxpr/reduce_sum | solution.py:64
  295.9 0.3 copy-done
  296.2 3.8 fusion.50
  300.2 0.1 le.66
  300.3 5.0 %fusion.47 = (f32[2048]{0:T(1024)S(1)}, f32[1024,2048]{1,0:T(8,128)}) fusion(s32[2048]{0:T(1024)S(1)} %le.66, s32[1024]{0:T(1024)S(1)} %bitcast.58, bf16[2048,128]{1,0:T(8,128)(2,1)} %get-tuple-element.211, bf16[8,1024,128]{2,1,0:T(8,128)(2,1)S(1)} %get-tuple-element.210, s32[]{:T(128)} %get-tuple-element.194), kind=kOutput, calls=%fused_computation.3.clone.1 | convolution fusion | flops 545257472 | bytes 9195524 | tf_op jit(solution)/shard_map/while/body/eval_jaxpr/dot_general | solution.py:58
  305.3 5.5 %fusion.48 = f32[2048]{0:T(1024)S(1)} fusion(f32[1024,2048]{1,0:T(8,128)} %get-tuple-element.180, f32[2048]{0:T(1024)S(1)} %select_maximum_fusion.2, s32[2048]{0:T(1024)S(1)} %le.66, s32[1024]{0:T(1024)S(1)} %bitcast.59), kind=kLoop, calls=%fused_computation.5.clone.1 | loop fusion | flops 12580864 | bytes 8417280 | tf_op jit(solution)/shard_map/while/body/eval_jaxpr/reduce_sum | solution.py:64
  310.9 0.3 copy-done
  311.2 3.8 fusion.50
  315.1 0.1 broadcast_in_dim.59
  315.2 0.1 le.66
  315.3 5.0 %fusion.47 = (f32[2048]{0:T(1024)S(1)}, f32[1024,2048]{1,0:T(8,128)}) fusion(s32[2048]{0:T(1024)S(1)} %le.66, s32[1024]{0:T(1024)S(1)} %bitcast.58, bf16[2048,128]{1,0:T(8,128)(2,1)} %get-tuple-element.211, bf16[8,1024,128]{2,1,0:T(8,128)(2,1)S(1)} %get-tuple-element.210, s32[]{:T(128)} %get-tuple-element.194), kind=kOutput, calls=%fused_computation.3.clone.1 | convolution fusion | flops 545257472 | bytes 9195524 | tf_op jit(solution)/shard_map/while/body/eval_jaxpr/dot_general | solution.py:58
  320.3 5.5 %fusion.48 = f32[2048]{0:T(1024)S(1)} fusion(f32[1024,2048]{1,0:T(8,128)} %get-tuple-element.180, f32[2048]{0:T(1024)S(1)} %select_maximum_fusion.2, s32[2048]{0:T(1024)S(1)} %le.66, s32[1024]{0:T(1024)S(1)} %bitcast.59), kind=kLoop, calls=%fused_computation.5.clone.1 | loop fusion | flops 12580864 | bytes 8417280 | tf_op jit(solution)/shard_map/while/body/eval_jaxpr/reduce_sum | solution.py:64
  325.9 0.3 copy-done
  326.2 3.8 fusion.50
  330.1 0.1 broadcast_in_dim.59
  330.2 0.1 le.66
  330.3 5.0 %fusion.47 = (f32[2048]{0:T(1024)S(1)}, f32[1024,2048]{1,0:T(8,128)}) fusion(s32[2048]{0:T(1024)S(1)} %le.66, s32[1024]{0:T(1024)S(1)} %bitcast.58, bf16[2048,128]{1,0:T(8,128)(2,1)} %get-tuple-element.211, bf16[8,1024,128]{2,1,0:T(8,128)(2,1)S(1)} %get-tuple-element.210, s32[]{:T(128)} %get-tuple-element.194), kind=kOutput, calls=%fused_computation.3.clone.1 | convolution fusion | flops 545257472 | bytes 9195524 | tf_op jit(solution)/shard_map/while/body/eval_jaxpr/dot_general | solution.py:58
  335.3 5.5 %fusion.48 = f32[2048]{0:T(1024)S(1)} fusion(f32[1024,2048]{1,0:T(8,128)} %get-tuple-element.180, f32[2048]{0:T(1024)S(1)} %select_maximum_fusion.2, s32[2048]{0:T(1024)S(1)} %le.66, s32[1024]{0:T(1024)S(1)} %bitcast.59), kind=kLoop, calls=%fused_computation.5.clone.1 | loop fusion | flops 12580864 | bytes 8417280 | tf_op jit(solution)/shard_map/while/body/eval_jaxpr/reduce_sum | solution.py:64
  340.9 0.3 copy-done
  341.2 3.8 fusion.50
  345.1 0.1 broadcast_in_dim.59
  345.2 0.1 le.66
  345.3 5.0 %fusion.47 = (f32[2048]{0:T(1024)S(1)}, f32[1024,2048]{1,0:T(8,128)}) fusion(s32[2048]{0:T(1024)S(1)} %le.66, s32[1024]{0:T(1024)S(1)} %bitcast.58, bf16[2048,128]{1,0:T(8,128)(2,1)} %get-tuple-element.211, bf16[8,1024,128]{2,1,0:T(8,128)(2,1)S(1)} %get-tuple-element.210, s32[]{:T(128)} %get-tuple-element.194), kind=kOutput, calls=%fused_computation.3.clone.1 | convolution fusion | flops 545257472 | bytes 9195524 | tf_op jit(solution)/shard_map/while/body/eval_jaxpr/dot_general | solution.py:58
  350.3 5.5 %fusion.48 = f32[2048]{0:T(1024)S(1)} fusion(f32[1024,2048]{1,0:T(8,128)} %get-tuple-element.180, f32[2048]{0:T(1024)S(1)} %select_maximum_fusion.2, s32[2048]{0:T(1024)S(1)} %le.66, s32[1024]{0:T(1024)S(1)} %bitcast.59), kind=kLoop, calls=%fused_computation.5.clone.1 | loop fusion | flops 12580864 | bytes 8417280 | tf_op jit(solution)/shard_map/while/body/eval_jaxpr/reduce_sum | solution.py:64
  355.9 0.3 copy-done
  356.2 3.8 fusion.50
  360.2 0.1 le.66
  360.3 5.0 %fusion.47 = (f32[2048]{0:T(1024)S(1)}, f32[1024,2048]{1,0:T(8,128)}) fusion(s32[2048]{0:T(1024)S(1)} %le.66, s32[1024]{0:T(1024)S(1)} %bitcast.58, bf16[2048,128]{1,0:T(8,128)(2,1)} %get-tuple-element.211, bf16[8,1024,128]{2,1,0:T(8,128)(2,1)S(1)} %get-tuple-element.210, s32[]{:T(128)} %get-tuple-element.194), kind=kOutput, calls=%fused_computation.3.clone.1 | convolution fusion | flops 545257472 | bytes 9195524 | tf_op jit(solution)/shard_map/while/body/eval_jaxpr/dot_general | solution.py:58
  365.3 5.5 %fusion.48 = f32[2048]{0:T(1024)S(1)} fusion(f32[1024,2048]{1,0:T(8,128)} %get-tuple-element.180, f32[2048]{0:T(1024)S(1)} %select_maximum_fusion.2, s32[2048]{0:T(1024)S(1)} %le.66, s32[1024]{0:T(1024)S(1)} %bitcast.59), kind=kLoop, calls=%fused_computation.5.clone.1 | loop fusion | flops 12580864 | bytes 8417280 | tf_op jit(solution)/shard_map/while/body/eval_jaxpr/reduce_sum | solution.py:64
  370.9 0.3 copy-done
  371.2 3.8 fusion.50
  375.1 0.1 broadcast_in_dim.59
  375.1 0.1 le.66
  375.3 5.0 %fusion.47 = (f32[2048]{0:T(1024)S(1)}, f32[1024,2048]{1,0:T(8,128)}) fusion(s32[2048]{0:T(1024)S(1)} %le.66, s32[1024]{0:T(1024)S(1)} %bitcast.58, bf16[2048,128]{1,0:T(8,128)(2,1)} %get-tuple-element.211, bf16[8,1024,128]{2,1,0:T(8,128)(2,1)S(1)} %get-tuple-element.210, s32[]{:T(128)} %get-tuple-element.194), kind=kOutput, calls=%fused_computation.3.clone.1 | convolution fusion | flops 545257472 | bytes 9195524 | tf_op jit(solution)/shard_map/while/body/eval_jaxpr/dot_general | solution.py:58
  380.3 5.5 %fusion.48 = f32[2048]{0:T(1024)S(1)} fusion(f32[1024,2048]{1,0:T(8,128)} %get-tuple-element.180, f32[2048]{0:T(1024)S(1)} %select_maximum_fusion.2, s32[2048]{0:T(1024)S(1)} %le.66, s32[1024]{0:T(1024)S(1)} %bitcast.59), kind=kLoop, calls=%fused_computation.5.clone.1 | loop fusion | flops 12580864 | bytes 8417280 | tf_op jit(solution)/shard_map/while/body/eval_jaxpr/reduce_sum | solution.py:64
  385.9 0.3 copy-done
  386.2 3.8 fusion.50
  390.1 0.1 le.66
  390.3 5.0 %fusion.47 = (f32[2048]{0:T(1024)S(1)}, f32[1024,2048]{1,0:T(8,128)}) fusion(s32[2048]{0:T(1024)S(1)} %le.66, s32[1024]{0:T(1024)S(1)} %bitcast.58, bf16[2048,128]{1,0:T(8,128)(2,1)} %get-tuple-element.211, bf16[8,1024,128]{2,1,0:T(8,128)(2,1)S(1)} %get-tuple-element.210, s32[]{:T(128)} %get-tuple-element.194), kind=kOutput, calls=%fused_computation.3.clone.1 | convolution fusion | flops 545257472 | bytes 9195524 | tf_op jit(solution)/shard_map/while/body/eval_jaxpr/dot_general | solution.py:58
  395.3 5.5 %fusion.48 = f32[2048]{0:T(1024)S(1)} fusion(f32[1024,2048]{1,0:T(8,128)} %get-tuple-element.180, f32[2048]{0:T(1024)S(1)} %select_maximum_fusion.2, s32[2048]{0:T(1024)S(1)} %le.66, s32[1024]{0:T(1024)S(1)} %bitcast.59), kind=kLoop, calls=%fused_computation.5.clone.1 | loop fusion | flops 12580864 | bytes 8417280 | tf_op jit(solution)/shard_map/while/body/eval_jaxpr/reduce_sum | solution.py:64
  400.9 0.3 copy-done
  401.2 3.8 fusion.50
  405.0 0.3 divide_convert_fusion
  405.4 0.2 all_to_all.14
  405.6 19.0 %all_to_all.19 = bf16[16,16,1024]{2,1,0:T(8,128)(2,1)S(1)} all-to-all(bf16[16,16,1024]{2,1,0:T(8,128)(2,1)S(1)} %all_to_all.14), channel_id=1, replica_groups=mesh['context'=32,'tensor'=16] {'tensor'}, dimensions={0} | all-to-all | bytes 1048576 | tf_op jit(solution)/shard_map/all_to_all | solution.py:98
  424.6 0.8 copy.7
  (55 shorter events, 0.7 us)
Async XLA Ops:
  6.5 86.9 %all-gather.7.cloned.1.call-start = ((), (), s32[]{:S(2)}) async-start(), calls=%async_computation.1 | async-start | bytes 1114112 | tf_op jit(solution)/shard_map/all_gather | solution.py:50
  7.3 186.6 %all-gather.9.cloned.1.call-start = ((), (), s32[]{:S(2)}) async-start(), calls=%async_computation.2 | async-start | bytes 2162688 | tf_op jit(solution)/shard_map/all_gather | solution.py:77
  95.0 190.0 %all-gather.11.cloned.1.call-start = ((), (), s32[]{:S(2)}) async-start(), calls=%async_computation.3 | async-start | bytes 2162688 | tf_op jit(solution)/shard_map/all_gather | solution.py:78
  213.3 71.7 %copy-start.1 = (s32[256]{0:T(256)S(1)}, s32[256]{0:T(256)}, u32[]{:S(2)}) copy-start(s32[256]{0:T(256)} %param.7) | copy-start | bytes 3076
  290.3 5.8 %copy-start = (f32[1024,2048]{1,0:T(8,128)S(1)}, f32[1024,2048]{1,0:T(8,128)}, u32[]{:S(2)}) copy-start(f32[1024,2048]{1,0:T(8,128)} %get-tuple-element.180) | copy-start | bytes 25165828 | tf_op jit(solution)/shard_map/while
  305.3 5.8 %copy-start = (f32[1024,2048]{1,0:T(8,128)S(1)}, f32[1024,2048]{1,0:T(8,128)}, u32[]{:S(2)}) copy-start(f32[1024,2048]{1,0:T(8,128)} %get-tuple-element.180) | copy-start | bytes 25165828 | tf_op jit(solution)/shard_map/while
  320.3 5.8 %copy-start = (f32[1024,2048]{1,0:T(8,128)S(1)}, f32[1024,2048]{1,0:T(8,128)}, u32[]{:S(2)}) copy-start(f32[1024,2048]{1,0:T(8,128)} %get-tuple-element.180) | copy-start | bytes 25165828 | tf_op jit(solution)/shard_map/while
  335.3 5.8 %copy-start = (f32[1024,2048]{1,0:T(8,128)S(1)}, f32[1024,2048]{1,0:T(8,128)}, u32[]{:S(2)}) copy-start(f32[1024,2048]{1,0:T(8,128)} %get-tuple-element.180) | copy-start | bytes 25165828 | tf_op jit(solution)/shard_map/while
  350.3 5.8 %copy-start = (f32[1024,2048]{1,0:T(8,128)S(1)}, f32[1024,2048]{1,0:T(8,128)}, u32[]{:S(2)}) copy-start(f32[1024,2048]{1,0:T(8,128)} %get-tuple-element.180) | copy-start | bytes 25165828 | tf_op jit(solution)/shard_map/while
  365.3 5.8 %copy-start = (f32[1024,2048]{1,0:T(8,128)S(1)}, f32[1024,2048]{1,0:T(8,128)}, u32[]{:S(2)}) copy-start(f32[1024,2048]{1,0:T(8,128)} %get-tuple-element.180) | copy-start | bytes 25165828 | tf_op jit(solution)/shard_map/while
  380.3 5.8 %copy-start = (f32[1024,2048]{1,0:T(8,128)S(1)}, f32[1024,2048]{1,0:T(8,128)}, u32[]{:S(2)}) copy-start(f32[1024,2048]{1,0:T(8,128)} %get-tuple-element.180) | copy-start | bytes 25165828 | tf_op jit(solution)/shard_map/while
  395.3 5.8 %copy-start = (f32[1024,2048]{1,0:T(8,128)S(1)}, f32[1024,2048]{1,0:T(8,128)}, u32[]{:S(2)}) copy-start(f32[1024,2048]{1,0:T(8,128)} %get-tuple-element.180) | copy-start | bytes 25165828 | tf_op jit(solution)/shard_map/while
Sparse Core Ops, SparseCore 0:
  9.4 83.9 all-gather.6
  96.8 97.0 all-gather.8
  197.2 87.7 all-gather.10
where the time goes:
time: 434 us; the launch traced here: 432 us
  waiting for transfers between devices  200 us (46%)
  matrix products  71.2 us (16%)
  blocking collectives  71 us (16%)
  other arithmetic  68.3 us (16%)
  between operations  13.2 us (3%)
  local copies, waits for them, and re-layouts  7.5 us (2%)
    all_gather x1, waiting for transfers between devices, local(): whole = lax.all_gather(key_value_rows, 'tensor', axis=1, tiled=True)  86.2 us
    all_gather x1, waiting for transfers between devices, local(): value_piece = lax.all_gather(value_rows, 'context', axis=0, tiled=True)  70.6 us
    all_gather x1, blocking collectives, local(): place_piece = lax.all_gather(positions, 'context', axis=0, tiled=True)  52 us
    reduce_sum x8, other arithmetic, attend(): new_sum = running_sum * factor + jnp.sum(weights, axis=1)  44.4 us
    all_gather x1, waiting for transfers between devices, local(): key_piece = lax.all_gather(key_rows, 'context', axis=0, tiled=True)  42 us
    dot_general x8, matrix products, attend(): jnp.dot(rotated_q, key_block.T, preferred_element_type=jnp.float32) * scale  40.4 us
    dot_general x8, matrix products, attend(): jnp.dot(weights.astype(jnp.bfloat16), value_block, preferred_element_type...  30.8 us
    another operation x1, other arithmetic  19.4 us
  transfers between devices with their start and end apart: 3, of which 3 were waited for; matrix products, arithmetic and copies ran while one was open for 6% of the time, Pallas kernels for 0%

commit v1 on v0

v1 whole, which is shorter than its diff:
```python
import functools
import math

import jax
import jax.numpy as jnp
import numpy as np
from jax import lax
from jax.experimental import pallas as pl
from jax.experimental.pallas import tpu as pltpu
from jax.sharding import PartitionSpec as P

HEAD = 128
BLOCK = 128
SLICE = 2 * BLOCK
NEGATIVE = -1e30
POSITIVE = 1e30
MESH = pl.DeviceIdType.MESH
F32 = jnp.float32
BF16 = jnp.bfloat16


LAYERS = ((0, 2 * BLOCK), (2 * BLOCK, 2 * BLOCK + 16))
SLOT = 4 * BLOCK + 16


def frequencies(width):
    counter = np.arange(width // 2, dtype=np.float32)
    inverse = np.float32(500000.0) ** (np.float32(-2.0) * counter / np.float32(width))
    wavelength = np.float32(2.0 * math.pi) / inverse
    smooth = np.clip((np.float32(8192.0) / wavelength - 1) / 3, 0, 1)
    f = (1 - smooth) * inverse / 8 + smooth * inverse
    return np.broadcast_to(np.concatenate([f, f])[None, :], (8, width)).astype(np.float32)


def dot_nn(a, b):
    return jnp.dot(a, b, preferred_element_type=F32)


def kernel(
    contexts, ranks, heads, block_rows,
    q_ref, kv_ref, place_ref, freq_ref, out_ref,
    queries, landed, slab, staged, qq, keys_one, keys_two, vals_big, vals_small, bias,
    out_big, out_small, max_big, max_small, done,
    q_sem, a_send, a_recv, m_send, m_recv, r_send, r_recv, s_send, s_recv, o_send, o_recv,
):
    ring = contexts // 4
    group = SLICE // ranks
    half_groups = ranks // 2
    plane = 2 * ranks
    blocks = 2 * contexts
    scale = math.log2(math.e) / math.sqrt(HEAD)

    c = lax.axis_index("context")
    t = lax.axis_index("tensor")
    core = lax.rem(c, 2)
    y = lax.rem(lax.div(c, 2), ring)
    z = lax.div(c, 2 * ring)
    way = 1 - 2 * core

    def at(zz, yy, cc):
        return (zz * ring + yy) * 2 + cc

    def turn(v):
        return lax.rem(v + 2 * ring, ring)

    following = at(z, turn(y + way), core)
    previous = at(z, turn(y - way), core)
    sibling = at(z, y, 1 - core)
    across = at(1 - z, y, core)
    me = z * ranks + t

    def near(k):
        pt = lax.rem(t + k, ranks)
        return z * ranks + pt, c, pt

    def far(k):
        pt = lax.rem(t + k, ranks)
        return (1 - z) * ranks + pt, across, pt

    barrier = pltpu.get_barrier_semaphore()

    def greet_near(k, carry):
        p, pc, pt = near(k)
        pl.semaphore_signal(barrier, inc=1, device_id=(pc, pt), device_id_type=MESH)
        return carry

    def greet_far(k, carry):
        p, pc, pt = far(k)
        pl.semaphore_signal(barrier, inc=1, device_id=(pc, pt), device_id_type=MESH)
        return carry

    lax.fori_loop(1, ranks, greet_near, 0)
    lax.fori_loop(0, ranks, greet_far, 0)
    for neighbour in (following, previous, sibling):
        pl.semaphore_signal(barrier, inc=1, device_id=(neighbour, t), device_id_type=MESH)

    fetch = pltpu.make_async_copy(q_ref, queries, q_sem.at[0])
    fetch.start()

    def number(half):
        return jnp.right_shift(place_ref[pl.ds(half, 1), :], 7).astype(F32)

    def rotation(block_number, start, rows):
        step = lax.broadcasted_iota(jnp.int32, (rows, HEAD), 0) + start
        angle = (block_number * BLOCK + step.astype(F32)) * freq_ref[0:1, :]
        lane = lax.broadcasted_iota(jnp.int32, (rows, HEAD), 1)
        return jnp.cos(angle), jnp.where(lane < HEAD // 2, -1.0, 1.0) * jnp.sin(angle)

    cos_k, sin_k = rotation(
        number(lax.div(t, half_groups)), lax.rem(t, half_groups) * group, group
    )
    for h in range(ranks // 2):
        cols = slice(h * HEAD, (h + 1) * HEAD)
        x = kv_ref[0, :, cols].astype(F32)
        staged[h, 0] = (x * cos_k + pltpu.roll(x, HEAD // 2, 1) * sin_k).astype(BF16)
        staged[h, 1] = kv_ref[1, :, cols]
    landed[z, 2 * ranks] = jnp.broadcast_to(number(0), (group, HEAD)).astype(BF16)
    mine_now = staged[lax.div(t, 2)]
    landed[z, 2 * t] = mine_now[0]
    landed[z, 2 * t + 1] = mine_now[1]

    pl.semaphore_wait(barrier, plane - 1 + 3)

    def plane_copy(peer):
        p, pc, pt = peer
        return pltpu.make_async_remote_copy(
            src_ref=staged.at[lax.div(pt, 2)],
            dst_ref=landed.at[z, pl.ds(2 * t, 2)],
            send_sem=a_send.at[p],
            recv_sem=a_recv.at[me],
            device_id=(pc, pt),
            device_id_type=MESH,
        )

    def near_start(k, carry):
        plane_copy(near(k)).start()
        return carry

    def far_start(k, carry):
        plane_copy(far(k)).start()
        return carry

    def id_copy(zz):
        return pltpu.make_async_remote_copy(
            src_ref=landed.at[zz, 2 * ranks],
            dst_ref=landed.at[zz, 2 * ranks],
            send_sem=m_send.at[0],
            recv_sem=m_recv.at[0],
            device_id=(across, t),
            device_id_type=MESH,
        )

    lax.fori_loop(1, ranks, near_start, 0)
    id_copy(z).start()
    lax.fori_loop(0, ranks, far_start, 0)

    def plane_wait(zz, pt):
        pltpu.make_async_remote_copy(
            src_ref=staged.at[0],
            dst_ref=landed.at[zz, pl.ds(2 * pt, 2)],
            send_sem=a_send.at[0],
            recv_sem=a_recv.at[zz * ranks + pt],
            device_id=(across, t),
            device_id_type=MESH,
        ).wait_recv()

    def near_wait(k, carry):
        plane_wait(z, lax.rem(t + k, ranks))
        return carry

    def far_wait(k, carry):
        plane_wait(1 - z, lax.rem(t + k, ranks))
        return carry

    def slot(r, s):
        return at(lax.rem(z + s, 2), turn(y - way * r), core)

    def slot_sibling(r, s):
        return at(lax.rem(z + s, 2), turn(y + way * r), 1 - core)

    def move(where, layer, send, recv, target):
        low, high = LAYERS[layer]
        view = slab.at[where, pl.ds(low, high)]
        return pltpu.make_async_remote_copy(
            src_ref=view, dst_ref=view, send_sem=send, recv_sem=recv,
            device_id=(target, t), device_id_type=MESH,
        )

    def ring_copy(r, s, layer):
        e = 2 * s + layer
        return move(slot(r, s), layer, r_send.at[r, e], r_recv.at[r + 1, e], following)

    def ring_wait(r, s, layer):
        e = 2 * s + layer
        move(slot(r, s), layer, r_send.at[r, e], r_recv.at[r, e], following).wait_recv()

    def sibling_copy(r, s, layer):
        e = 2 * s + layer
        return move(slot(r, s), layer, s_send.at[r, e], s_recv.at[r, e], sibling)

    def sibling_wait(r, s, layer):
        e = 2 * s + layer
        where = slot_sibling(r, s)
        move(where, layer, s_send.at[r, e], s_recv.at[r, e], sibling).wait_recv()

    def arrange(zz):
        where = at(zz, y, core)
        first = landed[zz, 2 * ranks].astype(F32)[0:1, :]
        smaller = first < blocks / 2
        halves = []
        for plane_index in range(2):
            pair = []
            for i in range(2):
                pieces = [
                    landed[zz, 2 * (i * half_groups + g) + plane_index] for g in range(half_groups)
                ]
                pair.append(jnp.concatenate(pieces, axis=0).astype(F32))
            halves.append(jnp.where(smaller, pair[0], pair[1]))
            halves.append(jnp.where(smaller, pair[1], pair[0]))
        slab[where, 0:BLOCK] = halves[0].T.astype(BF16)
        slab[where, BLOCK:2 * BLOCK] = halves[1].T.astype(BF16)
        slab[where, 2 * BLOCK:3 * BLOCK] = halves[2].astype(BF16)
        slab[where, 3 * BLOCK:4 * BLOCK] = halves[3].astype(BF16)
        low = jnp.minimum(first, blocks - 1 - first)
        slab[where, 4 * BLOCK:SLOT] = jnp.broadcast_to(low, (16, HEAD)).astype(BF16)

    def launch(s):
        for layer in range(2):
            ring_copy(0, s, layer).start()
            sibling_copy(0, s, layer).start()

    lax.fori_loop(1, ranks, near_wait, 0)
    arrange(z)
    launch(0)

    first_id = number(0)
    first_small = first_id < blocks / 2
    my_small = jnp.minimum(first_id, blocks - 1 - first_id)
    fetch.wait()
    turns = [rotation(number(i), 0, BLOCK) for i in range(2)]
    for h in range(heads):
        rows = slice(h * BLOCK, (h + 1) * BLOCK)
        turned = []
        for i in range(2):
            x = queries[i * BLOCK:(i + 1) * BLOCK, h * HEAD:(h + 1) * HEAD].astype(F32)
            turned.append(x * turns[i][0] + pltpu.roll(x, HEAD // 2, 1) * turns[i][1])
        qq[rows, 0:HEAD] = jnp.where(first_small, turned[0], turned[1]).astype(BF16)
        qq[rows, HEAD:2 * HEAD] = jnp.where(first_small, turned[1], turned[0]).astype(BF16)

    lax.fori_loop(0, ranks, far_wait, 0)
    id_copy(1 - z).wait_recv()
    arrange(1 - z)
    launch(1)

    ones = jnp.ones((BLOCK, HEAD), BF16)
    token = lax.broadcasted_iota(jnp.int32, (BLOCK, BLOCK), 0)
    key = lax.broadcasted_iota(jnp.int32, (BLOCK, BLOCK), 1)

    def diagonal(h, carry):
        rows = pl.ds(pl.multiple_of(h * BLOCK, BLOCK), BLOCK)
        for i, (best, total) in enumerate(((max_small, out_small), (max_big, out_big))):
            s = dot_nn(qq[rows, i * HEAD:(i + 1) * HEAD], slab[c, i * BLOCK:(i + 1) * BLOCK])
            s = jnp.where(key <= token, s, NEGATIVE)
            m = jnp.max(s, axis=1, keepdims=True)
            best[rows, :] = jnp.broadcast_to(m, (BLOCK, HEAD))
            values = jnp.concatenate(
                [slab[c, (2 + i) * BLOCK:(3 + i) * BLOCK], ones], axis=1
            )
            total[rows, :] = dot_nn(jnp.exp2((s - m) * scale).astype(BF16), values)
        return carry

    lax.fori_loop(0, heads, diagonal, 0)
    for i in range(4):
        vals_big[i * BLOCK:(i + 1) * BLOCK, HEAD:2 * HEAD] = ones

    def flag(condition):
        return jnp.where(condition, 1.0, 0.0)

    def prepare(r):
        places = (slot(r, 0), slot(r, 1), slot_sibling(r, 0), slot_sibling(r, 1))
        for i, where in enumerate(places):
            small = slab[where, 4 * BLOCK:SLOT].astype(F32)[0:1, :]
            low = flag(small < my_small)
            high = flag(small > my_small)
            bias[2 * i] = jnp.broadcast_to((high - 1.0) * POSITIVE, (8, HEAD))
            bias[2 * i + 1] = jnp.broadcast_to((low - 1.0) * POSITIVE, (8, HEAD))
            low = low.astype(BF16)
            high = high.astype(BF16)
            span = slice(i * BLOCK, (i + 1) * BLOCK)
            later = slice((4 + i) * BLOCK, (5 + i) * BLOCK)
            k_small = slab[where, 0:BLOCK]
            k_big = slab[where, BLOCK:2 * BLOCK]
            v_small = slab[where, 2 * BLOCK:3 * BLOCK]
            v_big = slab[where, 3 * BLOCK:4 * BLOCK]
            keys_one[:, span] = k_small
            keys_two[0:HEAD, span] = k_small * low
            keys_two[HEAD:2 * HEAD, span] = k_big * high
            vals_big[span, 0:HEAD] = v_small
            vals_big[later, 0:HEAD] = v_big * high
            vals_big[later, HEAD:2 * HEAD] = ones * high
            vals_small[span, 0:HEAD] = v_small * low
            vals_small[span, HEAD:2 * HEAD] = ones * low

    def advance(starts):
        bias_big = [bias[2 * i][0:1, :] for i in range(4)]
        bias_small = [bias[2 * i + 1][0:1, :] for i in range(4)]
        scores = []
        for start in starts:
            q = qq[start:start + block_rows, :]
            scores.append((dot_nn(q[:, HEAD:2 * HEAD], keys_one[...]), dot_nn(q, keys_two[...])))
        for start, (one, two) in zip(starts, scores):
            rows = slice(start, start + block_rows)
            ones_of = [one[:, i * BLOCK:(i + 1) * BLOCK] for i in range(4)]
            twos_of = [two[:, i * BLOCK:(i + 1) * BLOCK] for i in range(4)]
            big = functools.reduce(
                jnp.maximum, ones_of + [x + w for x, w in zip(twos_of, bias_big)]
            )
            small = functools.reduce(
                jnp.maximum, [x + w for x, w in zip(twos_of, bias_small)]
            )
            old_big = max_big[rows, :]
            old_small = max_small[rows, :]
            new_big = jnp.maximum(old_big, jnp.max(big, axis=1, keepdims=True))
            new_small = jnp.maximum(old_small, jnp.max(small, axis=1, keepdims=True))
            max_big[rows, :] = new_big
            max_small[rows, :] = new_small
            alpha_big = jnp.exp2((old_big - new_big) * scale)
            alpha_small = jnp.exp2((old_small - new_small) * scale)
            weights = [jnp.exp2((x - new_big) * scale).astype(BF16) for x in ones_of]
            later = []
            for x, wb, ws in zip(twos_of, bias_big, bias_small):
                m = jnp.where(wb == 0.0, new_big, jnp.where(ws == 0.0, new_small, POSITIVE))
                later.append(jnp.exp2((x - m) * scale).astype(BF16))
            later = jnp.concatenate(later, axis=1)
            every = jnp.concatenate(weights + [later], axis=1)
            wide_big = jnp.concatenate([alpha_big, alpha_big], axis=1)
            wide_small = jnp.concatenate([alpha_small, alpha_small], axis=1)
            out_big[rows, :] = out_big[rows, :] * wide_big + dot_nn(every, vals_big[...])
            out_small[rows, :] = out_small[rows, :] * wide_small + dot_nn(later, vals_small[...])

    half_heads = heads // 2
    width = half_heads * HEAD

    def columns(rank, s):
        return pl.ds(pl.multiple_of((2 * rank + s) * width, width), width)

    def tokens(rank):
        return pl.ds(pl.multiple_of(rank * group, group), group)

    def out_move(src, dst, s, send, recv, target):
        return pltpu.make_async_remote_copy(
            src_ref=done.at[tokens(src), pl.ds(s * width, width)],
            dst_ref=out_ref.at[:, columns(dst, s)],
            send_sem=o_send.at[send, s],
            recv_sem=o_recv.at[recv, s],
            device_id=(c, target),
            device_id_type=MESH,
        )

    def finish(s):
        for h in range(s * half_heads, (s + 1) * half_heads):
            rows = slice(h * BLOCK, (h + 1) * BLOCK)
            cols = slice(h * HEAD, (h + 1) * HEAD)
            small = out_small[rows, 0:HEAD] / out_small[rows, HEAD:2 * HEAD]
            big = out_big[rows, 0:HEAD] / out_big[rows, HEAD:2 * HEAD]
            done[0:BLOCK, cols] = jnp.where(first_small, small, big).astype(BF16)
            done[BLOCK:SLICE, cols] = jnp.where(first_small, big, small).astype(BF16)

        def out_start(k, carry):
            pt = lax.rem(t + k, ranks)
            out_move(pt, t, s, pt, t, pt).start()
            return carry

        lax.fori_loop(1, ranks, out_start, 0)
        out_ref[:, columns(t, s)] = done[tokens(t), s * width:(s + 1) * width]

    half_rows = heads * BLOCK // 2

    def step(r, carry):
        for s in range(2):
            for layer in range(2):
                sibling_wait(r, s, layer)
        prepare(r)
        for s in range(2):

            @pl.when(r < ring - 1)
            def _():
                for layer in range(2):
                    ring_wait(r + 1, s, layer)

                    @pl.when(r < ring - 2)
                    def _():
                        ring_copy(r + 1, s, layer).start()

                    sibling_copy(r + 1, s, layer).start()

            advance(range(s * half_rows, (s + 1) * half_rows, block_rows))

            @pl.when(r == ring - 1)
            def _():
                finish(s)

        return carry

    lax.fori_loop(0, ring, step, 0)

    def near_sent(k, carry):
        plane_copy(near(k)).wait_send()
        return carry

    def far_sent(k, carry):
        plane_copy(far(k)).wait_send()
        return carry

    def ring_sent(r, carry):
        for s in range(2):
            for layer in range(2):
                ring_copy(r, s, layer).wait_send()
        return carry

    def sibling_sent(r, carry):
        for s in range(2):
            for layer in range(2):
                sibling_copy(r, s, layer).wait_send()
        return carry

    def out_sent(k, carry):
        pt = lax.rem(t + k, ranks)
        for s in range(2):
            out_move(pt, t, s, pt, t, pt).wait_send()
        return carry

    def out_wait(k, carry):
        pt = lax.rem(t + k, ranks)
        for s in range(2):
            out_move(t, pt, s, t, pt, pt).wait_recv()
        return carry

    lax.fori_loop(1, ranks, near_sent, 0)
    lax.fori_loop(0, ranks, far_sent, 0)
    id_copy(z).wait_send()
    lax.fori_loop(0, ring - 1, ring_sent, 0)
    lax.fori_loop(0, ring, sibling_sent, 0)
    lax.fori_loop(1, ranks, out_sent, 0)
    lax.fori_loop(1, ranks, out_wait, 0)


def local(contexts, ranks, queries, key_value_rows, positions):
    heads = queries.shape[1] // HEAD
    group = SLICE // ranks
    ring = contexts // 4
    rows = heads * BLOCK
    block_rows = min(256, rows // 4)
    dma = pltpu.SemaphoreType.DMA
    vmem = pl.BlockSpec(memory_space=pltpu.VMEM)
    return pl.pallas_call(
        functools.partial(kernel, contexts, ranks, heads, block_rows),
        out_shape=jax.ShapeDtypeStruct((group, ranks * heads * HEAD), BF16),
        in_specs=[pl.BlockSpec(memory_space=pl.ANY), vmem, vmem, vmem],
        out_specs=vmem,
        scratch_shapes=[
            pltpu.VMEM((SLICE, heads * HEAD), BF16),
            pltpu.VMEM((2, 2 * ranks + 1, group, HEAD), BF16),
            pltpu.VMEM((contexts, SLOT, HEAD), BF16),
            pltpu.VMEM((ranks // 2, 2, group, HEAD), BF16),
            pltpu.VMEM((rows, 2 * HEAD), BF16),
            pltpu.VMEM((HEAD, 4 * BLOCK), BF16),
            pltpu.VMEM((2 * HEAD, 4 * BLOCK), BF16),
            pltpu.VMEM((8 * BLOCK, 2 * HEAD), BF16),
            pltpu.VMEM((4 * BLOCK, 2 * HEAD), BF16),
            pltpu.VMEM((8, 8, HEAD), F32),
            pltpu.VMEM((rows, 2 * HEAD), F32),
            pltpu.VMEM((rows, 2 * HEAD), F32),
            pltpu.VMEM((rows, HEAD), F32),
            pltpu.VMEM((rows, HEAD), F32),
            pltpu.VMEM((SLICE, heads * HEAD), BF16),
            dma((1,)),
            dma((2 * ranks,)),
            dma((2 * ranks,)),
            dma((1,)),
            dma((1,)),
            dma((ring, 4)),
            dma((ring, 4)),
            dma((ring, 4)),
            dma((ring, 4)),
            dma((ranks, 2)),
            dma((ranks, 2)),
        ],
        compiler_params=pltpu.CompilerParams(
            collective_id=0, has_side_effects=True, vmem_limit_bytes=48 * 1024 * 1024
        ),
        cost_estimate=pl.CostEstimate(
            flops=8 * rows * SLICE * contexts * HEAD // 2,
            bytes_accessed=4 * 1024 * 1024,
            transcendentals=rows * SLICE * contexts,
        ),
    )(queries, key_value_rows, positions.reshape(2, BLOCK), jnp.asarray(frequencies(HEAD)))


def solution(mesh):
    placed = (P("context", "tensor"), P(None, ("context", "tensor"), None), P("context"))
    return jax.shard_map(
        functools.partial(local, mesh.shape["context"], mesh.shape["tensor"]),
        mesh=mesh,
        in_specs=placed,
        out_specs=P(("context", "tensor"), None),
        check_vma=False,
    )
```

time: 434 us -> 74.8 us (0.17)
  waiting for transfers between devices: 200 us -> 0 us
  matrix products: 71.2 us -> 0 us
  blocking collectives: 71 us -> 0 us
  Pallas kernels: 0 us -> 69.3 us
  other arithmetic: 68.3 us -> 0 us
  between operations: 13.2 us -> 0.01 us
    all_gather x3 -> x0, waiting for transfers between devices: 199 us -> none  [the longest x1 86.2 us: local(): whole = lax.all_gather(key_value_rows, 'tensor', axis=1, tiled=True)]
    dot_general x16 -> x0, matrix products: 71.2 us -> none  [the longest x8 40.4 us: attend(): jnp.dot(rotated_q, key_block.T, preferred_element_type=jnp.float32) * scale]
    pallas_call x0 -> x1, Pallas kernels: none -> 69.3 us  [local(): pl.pallas_call(functools.partial(kernel, contexts, ranks, heads, block_ro...]
    all_gather x1 -> x0, blocking collectives: 52 us -> none  [local(): place_piece = lax.all_gather(positions, 'context', axis=0, tiled=True)]
    reduce_sum x8 -> x0, other arithmetic: 44.4 us -> none  [attend(): new_sum = running_sum * factor + jnp.sum(weights, axis=1)]
    another operation x1 -> x0, other arithmetic: 19.4 us -> none
    all_to_all x1 -> x0, blocking collectives: 19 us -> none  [local(): lax.all_to_all(heads, 'tensor', split_axis=0, concat_axis=1, tiled=True)]
  transfers between devices with their start and end apart: 3 -> 0, of which waited for: 3 -> 0; matrix products, arithmetic and copies ran while one was open for 6% -> 0% of each run, Pallas kernels for 0% -> 0%
where the time goes in v1:
time: 74.8 us; the launch traced here: 73.3 us
  Pallas kernels  69.3 us (93%)
  local copies, waits for them, and re-layouts  4.04 us (5%)
    pallas_call x1, Pallas kernels, local(): pl.pallas_call(functools.partial(kernel, contexts, ranks, heads, block_ro...  69.3 us
    unnamed x9, local copies, waits for them, and re-layouts  4.04 us

profile of v1, /device:TPU:6, one launch (start us, length us, event | category | flops | bytes accessed | tf_op | source)
XLA Modules:
  0.0 73.3 jit_solution(14343385630689886973)
XLA Ops:
  0.0 0.0 copy-start.2
  0.0 0.7 copy-done.2
  0.7 0.0 copy-start
  0.7 1.0 %copy-done = bf16[256,1024]{1,0:T(8,128)(2,1)S(1)} copy-done((bf16[256,1024]{1,0:T(8,128)(2,1)S(1)}, bf16[256,1024]{1,0:T(8,128)(2,1)}, u32[]{:S(2)}) %copy-start) | copy-done | bytes 524312
  1.7 0.0 copy-start.1
  1.7 0.8 %copy-done.1 = bf16[2,16,1024]{2,1,0:T(8,128)(2,1)S(1)} copy-done((bf16[2,16,1024]{2,1,0:T(8,128)(2,1)S(1)}, bf16[2,16,1024]{2,1,0:T(8,128)(2,1)}, u32[]{:S(2)}) %copy-start.1) | copy-done | bytes 65560
  2.6 0.0 copy-start.3
  2.6 0.7 copy-done.3
  3.2 69.3 %shard_map.46 = bf16[16,16384]{1,0:T(8,128)(2,1)S(1)} custom-call(bf16[256,1024]{1,0:T(8,128)(2,1)S(1)} %copy-done, bf16[2,16,1024]{2,1,0:T(8,128)(2,1)S(1)} %copy-done.1, s32[2,128]{1,0:T(2,128)S(1)} %bitcast.1, f32[8,128]{1,0:T(8,128)S(1)} %copy-done.3), custom_call_target="tpu_custom_call" | custom-call | flops 4294967296 | bytes 4194304 | tf_op jit(solution)/shard_map/pallas_call | solution.py:456
  72.5 0.8 %copy.6 = bf16[16,16384]{1,0:T(8,128)(2,1)} copy(bf16[16,16384]{1,0:T(8,128)(2,1)S(1)} %shard_map.46) | data formatting | bytes 1048576
Async XLA Ops:
  0.0 0.7 copy-start.2
  0.7 1.0 %copy-start = (bf16[256,1024]{1,0:T(8,128)(2,1)S(1)}, bf16[256,1024]{1,0:T(8,128)(2,1)}, u32[]{:S(2)}) copy-start(bf16[256,1024]{1,0:T(8,128)(2,1)} %q_ref.1) | copy-start | bytes 1572868
  1.7 0.8 %copy-start.1 = (bf16[2,16,1024]{2,1,0:T(8,128)(2,1)S(1)}, bf16[2,16,1024]{2,1,0:T(8,128)(2,1)}, u32[]{:S(2)}) copy-start(bf16[2,16,1024]{2,1,0:T(8,128)(2,1)} %kv_ref.1) | copy-start | bytes 196612
  2.6 0.7 copy-start.3

commit v2 on v1

v2 whole, which is shorter than its diff:
```python
import functools
import math

import jax
import jax.numpy as jnp
import numpy as np
from jax import lax
from jax.experimental import pallas as pl
from jax.experimental.pallas import tpu as pltpu
from jax.sharding import PartitionSpec as P

HEAD = 128
BLOCK = 128
SLICE = 2 * BLOCK
NEGATIVE = -1e30
POSITIVE = 1e30
MESH = pl.DeviceIdType.MESH
F32 = jnp.float32
BF16 = jnp.bfloat16


LAYERS = ((0, 2 * BLOCK + 16), (2 * BLOCK + 16, 2 * BLOCK))
NUMBER = 2 * BLOCK
BIG = 2 * BLOCK + 16
SLOT = 4 * BLOCK + 16


def frequencies(width):
    counter = np.arange(width // 2, dtype=np.float32)
    inverse = np.float32(500000.0) ** (np.float32(-2.0) * counter / np.float32(width))
    wavelength = np.float32(2.0 * math.pi) / inverse
    smooth = np.clip((np.float32(8192.0) / wavelength - 1) / 3, 0, 1)
    f = (1 - smooth) * inverse / 8 + smooth * inverse
    return np.broadcast_to(np.concatenate([f, f])[None, :], (8, width)).astype(np.float32)


def dot_nn(a, b):
    return jnp.dot(a, b, preferred_element_type=F32)


def kernel(
    contexts, ranks, heads, block_rows,
    q_hbm, kv_hbm, place_hbm, freq_hbm, out_ref,
    queries, kv_ref, place_ref, freq_ref, landed, numbers, slab, staged, crossed,
    qq, keys_one, keys_two, vals_one, vals_two, vals_small, bias,
    out_big, out_small, max_big, max_small, part_out, part_in, sums_out, sums_in, done,
    in_sem, x_send, x_recv, z_send, z_recv, m_send, m_recv, r_send, r_recv, g_send, g_recv, p_send, p_recv, o_send, o_recv, k_sem,
):
    ring = contexts // 4
    group = SLICE // ranks
    half_groups = ranks // 2
    wide = min(4, ranks)
    deep = ranks // wide
    blocks = 2 * contexts
    scale = math.log2(math.e) / math.sqrt(HEAD)
    total = heads * BLOCK

    c = lax.axis_index("context")
    t = lax.axis_index("tensor")
    core = lax.rem(c, 2)
    y = lax.rem(lax.div(c, 2), ring)
    z = lax.div(c, 2 * ring)
    half_ring = ring // 2

    def at(zz, yy, cc):
        return (zz * ring + yy) * 2 + cc

    def turn(v):
        return lax.rem(v + 2 * ring, ring)

    after = at(z, turn(y + 1), core)
    before = at(z, turn(y + ring - 1), core)
    sibling = at(z, y, 1 - core)
    across = at(1 - z, y, core)
    x = lax.rem(t, wide)
    low_z = lax.div(t, wide)

    def row_peer(k):
        return low_z * wide + lax.rem(x + k, wide)

    def near_peer(k):
        return lax.rem(low_z + k, deep) * wide + x

    fetches = [
        pltpu.make_async_copy(src, dst, in_sem.at[i])
        for i, (src, dst) in enumerate((
            (place_hbm, place_ref), (freq_hbm, freq_ref), (kv_hbm, kv_ref), (q_hbm, queries)
        ))
    ]
    for fetch in fetches:
        fetch.start()

    barrier = pltpu.get_barrier_semaphore()

    def greet_group(k, carry):
        pl.semaphore_signal(
            barrier, inc=1, device_id=(c, lax.rem(t + k, ranks)), device_id_type=MESH
        )
        return carry

    def greet_far(k, carry):
        pl.semaphore_signal(
            barrier, inc=1, device_id=(across, near_peer(k)), device_id_type=MESH
        )
        return carry

    lax.fori_loop(1, ranks, greet_group, 0)
    lax.fori_loop(0, deep, greet_far, 0)
    for neighbour in (after, before, sibling):
        pl.semaphore_signal(barrier, inc=1, device_id=(neighbour, t), device_id_type=MESH)

    def number(half):
        return jnp.right_shift(place_ref[pl.ds(half, 1), :], 7).astype(F32)

    def rotation(block_number, start, rows):
        step = lax.broadcasted_iota(jnp.int32, (rows, HEAD), 0) + start
        angle = (block_number * BLOCK + step.astype(F32)) * freq_ref[0:1, :]
        lane = lax.broadcasted_iota(jnp.int32, (rows, HEAD), 1)
        return jnp.cos(angle), jnp.where(lane < HEAD // 2, -1.0, 1.0) * jnp.sin(angle)

    for fetch in fetches[:3]:
        fetch.wait()
    cos_k, sin_k = rotation(
        number(lax.div(t, half_groups)), lax.rem(t, half_groups) * group, group
    )
    for h in range(ranks // 2):
        cols = slice(h * HEAD, (h + 1) * HEAD)
        place = (h % (wide // 2), h // (wide // 2))
        value = kv_ref[0, :, cols].astype(F32)
        turned = value * cos_k + pltpu.roll(value, HEAD // 2, 1) * sin_k
        staged[place[0], place[1], 0] = turned.astype(BF16)
        staged[place[0], place[1], 1] = kv_ref[1, :, cols]
    numbers[z] = jnp.broadcast_to(number(0), (16, HEAD)).astype(BF16)

    pl.semaphore_wait(barrier, ranks - 1 + deep + 3)

    def row_copy(k):
        peer = row_peer(k)
        return pltpu.make_async_remote_copy(
            src_ref=staged.at[lax.div(lax.rem(peer, wide), 2)],
            dst_ref=crossed.at[x],
            send_sem=x_send.at[k],
            recv_sem=x_recv.at[x],
            device_id=(c, peer),
            device_id_type=MESH,
        )

    def row_wait(k):
        pltpu.make_async_remote_copy(
            src_ref=staged.at[0],
            dst_ref=crossed.at[lax.rem(x + k, wide)],
            send_sem=x_send.at[k],
            recv_sem=x_recv.at[lax.rem(x + k, wide)],
            device_id=(c, row_peer(k)),
            device_id_type=MESH,
        ).wait_recv()

    def column_copy(k, target, part):
        peer = near_peer(k)
        return pltpu.make_async_remote_copy(
            src_ref=crossed.at[:, lax.div(peer, wide)],
            dst_ref=landed.at[z, pl.ds(low_z * wide, wide)],
            send_sem=z_send.at[part, k],
            recv_sem=z_recv.at[z, low_z],
            device_id=(target, peer),
            device_id_type=MESH,
        )

    def column_wait(zz, k):
        source = lax.rem(low_z + k, deep)
        pltpu.make_async_remote_copy(
            src_ref=crossed.at[:, 0],
            dst_ref=landed.at[zz, pl.ds(source * wide, wide)],
            send_sem=z_send.at[0, 0],
            recv_sem=z_recv.at[zz, source],
            device_id=(across, t),
            device_id_type=MESH,
        ).wait_recv()

    def id_copy(zz):
        return pltpu.make_async_remote_copy(
            src_ref=numbers.at[zz],
            dst_ref=numbers.at[zz],
            send_sem=m_send.at[0],
            recv_sem=m_recv.at[0],
            device_id=(across, t),
            device_id_type=MESH,
        )

    for k in range(1, wide):
        row_copy(k).start()
    id_copy(z).start()
    crossed[x] = staged[lax.div(x, 2)]
    for k in range(1, wide):
        row_wait(k)
    for k in range(1, deep):
        column_copy(k, c, 0).start()
    for k in range(deep):
        column_copy(k, across, 1).start()
    landed[z, pl.ds(low_z * wide, wide)] = crossed[:, low_z]

    def slot(k, way, s):
        return at(lax.rem(z + s, 2), turn(y + ring - (1 - 2 * way) * k), core)

    def move(where, layer, send, recv, target):
        low, size = LAYERS[layer]
        view = slab.at[where, pl.ds(low, size)]
        return pltpu.make_async_remote_copy(
            src_ref=view, dst_ref=view, send_sem=send, recv_sem=recv,
            device_id=(target, t), device_id_type=MESH,
        )

    def entry(way, s, layer):
        return 4 * way + 2 * s + layer

    def ring_copy(k, way, s, layer):
        e = entry(way, s, layer)
        target = at(z, turn(y + ring + 1 - 2 * way), core)
        return move(
            slot(k, way, s), layer, r_send.at[k, e], r_recv.at[k + 1, e], target
        )

    def ring_wait(k, way, s, layer):
        e = entry(way, s, layer)
        move(
            slot(k, way, s), layer, r_send.at[k, e], r_recv.at[k, e], after
        ).wait_recv()

    def goes_on(k, way, s):
        return jnp.logical_or(k < half_ring - 1, jnp.logical_and(k == half_ring - 1, s == way))

    def arrive(k, s, layer):
        for way in range(2):

            @pl.when(goes_on(k - 1, way, s))
            def _():
                ring_wait(k, way, s, layer)

                @pl.when(goes_on(k, way, s))
                def _():
                    ring_copy(k, way, s, layer).start()

    def arrange(zz):
        where = at(zz, y, core)
        first = numbers[zz].astype(F32)[0:1, :]
        smaller = first < blocks / 2
        halves = []
        for plane_index in range(2):
            pair = []
            for i in range(2):
                pieces = [
                    landed[zz, i * half_groups + g, plane_index] for g in range(half_groups)
                ]
                pair.append(jnp.concatenate(pieces, axis=0).astype(F32))
            halves.append(jnp.where(smaller, pair[0], pair[1]))
            halves.append(jnp.where(smaller, pair[1], pair[0]))
        slab[where, 0:BLOCK] = halves[0].T.astype(BF16)
        slab[where, BLOCK:2 * BLOCK] = halves[2].astype(BF16)
        low = jnp.minimum(first, blocks - 1 - first)
        slab[where, NUMBER:NUMBER + 16] = jnp.broadcast_to(low, (16, HEAD)).astype(BF16)
        slab[where, BIG:BIG + BLOCK] = halves[1].T.astype(BF16)
        slab[where, BIG + BLOCK:SLOT] = halves[3].astype(BF16)

    def launch(s):
        for layer in range(2):
            for way in range(2):
                if half_ring > 1 or s == way:
                    ring_copy(0, way, s, layer).start()

    first_id = number(0)
    first_small = first_id < blocks / 2
    fetches[3].wait()
    turns = [rotation(number(i), 0, BLOCK) for i in range(2)]
    for h in range(heads):
        rows = slice(h * BLOCK, (h + 1) * BLOCK)
        turned = []
        for i in range(2):
            value = queries[i * BLOCK:(i + 1) * BLOCK, h * HEAD:(h + 1) * HEAD].astype(F32)
            turned.append(value * turns[i][0] + pltpu.roll(value, HEAD // 2, 1) * turns[i][1])
        qq[1, rows, 0:HEAD] = jnp.where(first_small, turned[0], turned[1]).astype(BF16)
        qq[1, rows, HEAD:2 * HEAD] = jnp.where(first_small, turned[1], turned[0]).astype(BF16)
    qq[1, total:total + 16, :] = jnp.broadcast_to(
        jnp.concatenate([first_id, first_id], axis=1), (16, 2 * HEAD)
    ).astype(BF16)
    swap = pltpu.make_async_remote_copy(
        src_ref=qq.at[1], dst_ref=qq.at[0], send_sem=g_send.at[0], recv_sem=g_recv.at[0],
        device_id=(sibling, t), device_id_type=MESH,
    )
    swap.start()

    for k in range(1, deep):
        column_wait(z, k)
    arrange(z)
    launch(0)

    for k in range(deep):
        column_wait(1 - z, k)
    id_copy(1 - z).wait_recv()
    arrange(1 - z)
    launch(1)

    for best in (max_small, max_big):
        best[0] = jnp.full((total, HEAD), NEGATIVE, F32)
    for sums in (out_small, out_big):
        sums[0] = jnp.zeros((total, 2 * HEAD), F32)
    ones = jnp.ones((BLOCK, HEAD), BF16)
    token = lax.broadcasted_iota(jnp.int32, (BLOCK, BLOCK), 0)
    key = lax.broadcasted_iota(jnp.int32, (BLOCK, BLOCK), 1)

    def diagonal(h, carry):
        rows = pl.ds(pl.multiple_of(h * BLOCK, BLOCK), BLOCK)
        for i, (best, sums) in enumerate(((max_small, out_small), (max_big, out_big))):
            s = dot_nn(qq[1, rows, i * HEAD:(i + 1) * HEAD], slab[c, i * BIG:i * BIG + BLOCK])
            s = jnp.where(key <= token, s, NEGATIVE)
            m = jnp.max(s, axis=1, keepdims=True)
            best[1, rows, :] = jnp.broadcast_to(m, (BLOCK, HEAD))
            values = jnp.concatenate(
                [slab[c, i * BIG + BLOCK:i * BIG + 2 * BLOCK], ones], axis=1
            )
            sums[1, rows, :] = dot_nn(jnp.exp2((s - m) * scale).astype(BF16), values)
        return carry

    lax.fori_loop(0, heads, diagonal, 0)
    for i in range(4):
        vals_one[i * BLOCK:(i + 1) * BLOCK, HEAD:2 * HEAD] = ones

    def flag(condition):
        return jnp.where(condition, 1.0, 0.0)

    def prepare(places, owner):
        asker = qq[owner, total:total + 16, 0:HEAD].astype(F32)[0:1, :]
        my_small = jnp.minimum(asker, blocks - 1 - asker)
        for i, where in enumerate(places):
            small = slab[where, NUMBER:NUMBER + 16].astype(F32)[0:1, :]
            low = flag(small < my_small)
            high = flag(small > my_small)
            bias[2 * i] = jnp.broadcast_to((high - 1.0) * POSITIVE, (8, HEAD))
            bias[2 * i + 1] = jnp.broadcast_to((low - 1.0) * POSITIVE, (8, HEAD))
            low = low.astype(BF16)
            high = high.astype(BF16)
            span = slice(i * BLOCK, (i + 1) * BLOCK)
            k_small = slab[where, 0:BLOCK]
            k_big = slab[where, BIG:BIG + BLOCK]
            v_small = slab[where, BLOCK:2 * BLOCK]
            v_big = slab[where, BIG + BLOCK:SLOT]
            keys_one[:, span] = k_small
            keys_two[0:HEAD, span] = k_small * low
            keys_two[HEAD:2 * HEAD, span] = k_big * high
            vals_one[span, 0:HEAD] = v_small
            vals_two[span, 0:HEAD] = v_big * high
            vals_two[span, HEAD:2 * HEAD] = ones * high
            vals_small[span, 0:HEAD] = v_small * low
            vals_small[span, HEAD:2 * HEAD] = ones * low

    def advance(n, owner, s):
        starts = range(s * half_rows, (s + 1) * half_rows, block_rows)
        keys = slice(0, n * BLOCK)
        bias_big = [bias[2 * i][0:1, :] for i in range(n)]
        bias_small = [bias[2 * i + 1][0:1, :] for i in range(n)]
        scores = []
        for start in starts:
            q = qq[owner, start:start + block_rows, :]
            scores.append((
                dot_nn(q[:, HEAD:2 * HEAD], keys_one[:, keys]), dot_nn(q, keys_two[:, keys])
            ))
        for start, (one, two) in zip(starts, scores):
            rows = slice(start, start + block_rows)
            ones_of = [one[:, i * BLOCK:(i + 1) * BLOCK] for i in range(n)]
            twos_of = [two[:, i * BLOCK:(i + 1) * BLOCK] for i in range(n)]
            big = functools.reduce(
                jnp.maximum, ones_of + [x + w for x, w in zip(twos_of, bias_big)]
            )
            small = functools.reduce(
                jnp.maximum, [x + w for x, w in zip(twos_of, bias_small)]
            )
            old_big = max_big[owner, rows, :]
            old_small = max_small[owner, rows, :]
            new_big = jnp.maximum(old_big, jnp.max(big, axis=1, keepdims=True))
            new_small = jnp.maximum(old_small, jnp.max(small, axis=1, keepdims=True))
            max_big[owner, rows, :] = new_big
            max_small[owner, rows, :] = new_small
            alpha_big = jnp.exp2((old_big - new_big) * scale)
            alpha_small = jnp.exp2((old_small - new_small) * scale)
            weights = [jnp.exp2((x - new_big) * scale).astype(BF16) for x in ones_of]
            later = []
            for x, wb, ws in zip(twos_of, bias_big, bias_small):
                m = jnp.where(wb == 0.0, new_big, jnp.where(ws == 0.0, new_small, POSITIVE))
                later.append(jnp.exp2((x - m) * scale).astype(BF16))
            later = jnp.concatenate(later, axis=1)
            every = jnp.concatenate(weights + [later], axis=1)
            values = jnp.concatenate([vals_one[keys, :], vals_two[keys, :]], axis=0)
            wide_big = jnp.concatenate([alpha_big, alpha_big], axis=1)
            wide_small = jnp.concatenate([alpha_small, alpha_small], axis=1)
            out_big[owner, rows, :] = out_big[owner, rows, :] * wide_big + dot_nn(every, values)
            out_small[owner, rows, :] = (
                out_small[owner, rows, :] * wide_small + dot_nn(later, vals_small[keys, :])
            )

    half_heads = heads // 2
    half_rows = total // 2

    lane = lax.broadcasted_iota(jnp.int32, (BLOCK, HEAD), 1)
    log2_e = math.log2(math.e)

    def log_sum(best, weight):
        return best * scale + jnp.log(weight) * log2_e

    def part_copy(i):
        if i == 2:
            src, dst = sums_out, sums_in
        else:
            src = part_out.at[pl.ds(i * half_rows, half_rows)]
            dst = part_in.at[pl.ds(i * half_rows, half_rows)]
        return pltpu.make_async_remote_copy(
            src_ref=src, dst_ref=dst, send_sem=p_send.at[i], recv_sem=p_recv.at[i],
            device_id=(sibling, t), device_id_type=MESH,
        )

    def give_back(s):
        packed = jnp.zeros((BLOCK, HEAD), F32) if s == 0 else sums_out[...]
        for h in range(s * half_heads, (s + 1) * half_heads):
            rows = slice(h * BLOCK, (h + 1) * BLOCK)
            for i, (best, sums) in enumerate(((max_small, out_small), (max_big, out_big))):
                weight = jnp.maximum(sums[0, rows, HEAD:2 * HEAD], 1.0)
                part_out[rows, i * HEAD:(i + 1) * HEAD] = (
                    sums[0, rows, 0:HEAD] / weight
                ).astype(BF16)
                first = h * 16 + i * 8
                inside = jnp.logical_and(lane >= first, lane < first + 8)
                packed = jnp.where(inside, log_sum(best[0, rows, :], weight), packed)
        sums_out[...] = packed
        part_copy(s).start()

    width = half_heads * HEAD

    def columns(rank, s):
        return pl.ds(pl.multiple_of((2 * rank + s) * width, width), width)

    def tokens(rank):
        return pl.ds(pl.multiple_of(rank * group, group), group)

    def out_move(src, dst, s, send, recv, target):
        return pltpu.make_async_remote_copy(
            src_ref=done.at[tokens(src), pl.ds(s * width, width)],
            dst_ref=out_ref.at[:, columns(dst, s)],
            send_sem=o_send.at[send, s],
            recv_sem=o_recv.at[recv, s],
            device_id=(c, target),
            device_id_type=MESH,
        )

    def out_keep(s):
        return pltpu.make_async_copy(
            done.at[tokens(t), pl.ds(s * width, width)], out_ref.at[:, columns(t, s)], k_sem.at[s]
        )

    def finish(s):
        for h in range(s * half_heads, (s + 1) * half_heads):
            rows = slice(h * BLOCK, (h + 1) * BLOCK)
            cols = slice(h * HEAD, (h + 1) * HEAD)
            merged = []
            for i, (best, sums) in enumerate(((max_small, out_small), (max_big, out_big))):
                weight = sums[1, rows, HEAD:2 * HEAD]
                mine = log_sum(best[1, rows, :], weight)
                first = h * 16 + i * 8
                theirs = jnp.broadcast_to(sums_in[:, first:first + 1], (BLOCK, HEAD))
                top = jnp.maximum(mine, theirs)
                mine = jnp.exp2(mine - top)
                theirs = jnp.exp2(theirs - top)
                other_part = part_in[rows, i * HEAD:(i + 1) * HEAD].astype(F32)
                value = sums[1, rows, 0:HEAD] * (mine / weight) + other_part * theirs
                merged.append(value / (mine + theirs))
            small, big = merged
            done[0:BLOCK, cols] = jnp.where(first_small, small, big).astype(BF16)
            done[BLOCK:SLICE, cols] = jnp.where(first_small, big, small).astype(BF16)

        def out_start(k, carry):
            pt = lax.rem(t + k, ranks)
            out_move(pt, t, s, pt, t, pt).start()
            return carry

        lax.fori_loop(1, ranks, out_start, 0)
        out_keep(s).start()

    def attend(k, ways, owner):
        prepare([slot(k, way, s) for way in ways for s in range(2)], owner)
        for s in range(2):
            advance(2 * len(ways), owner, s)
            arrive(k + 1, owner, s)

    swap.wait_recv()

    def first_step(owner, carry):
        attend(0, (0,), owner)
        return carry

    lax.fori_loop(0, 2, first_step, 0)

    def step(i, carry):
        attend(lax.div(i, 2) + 1, (0, 1), lax.rem(i, 2))
        return carry

    if half_ring > 1:
        lax.fori_loop(0, 2 * (half_ring - 1), step, 0)

    last = [slot(half_ring, 0, s) for s in range(2)]
    prepare(last, 0)
    for s in range(2):
        advance(2, 0, s)
        give_back(s)
    part_copy(2).start()
    prepare(last, 1)
    advance(2, 1, 0)
    part_copy(2).wait_recv()
    part_copy(0).wait_recv()
    finish(0)
    advance(2, 1, 1)
    part_copy(1).wait_recv()
    finish(1)

    def ring_sent(k, carry):
        for way in range(2):
            for s in range(2):
                for layer in range(2):

                    @pl.when(goes_on(k, way, s))
                    def _():
                        ring_copy(k, way, s, layer).wait_send()

        return carry

    def out_sent(k, carry):
        pt = lax.rem(t + k, ranks)
        for s in range(2):
            out_move(pt, t, s, pt, t, pt).wait_send()
        return carry

    def out_wait(k, carry):
        pt = lax.rem(t + k, ranks)
        for s in range(2):
            out_move(t, pt, s, t, pt, pt).wait_recv()
        return carry

    for k in range(1, wide):
        row_copy(k).wait_send()
    for k in range(1, deep):
        column_copy(k, c, 0).wait_send()
    for k in range(deep):
        column_copy(k, across, 1).wait_send()
    id_copy(z).wait_send()
    lax.fori_loop(0, half_ring, ring_sent, 0)
    swap.wait_send()
    for i in range(3):
        part_copy(i).wait_send()
    for s in range(2):
        out_keep(s).wait()
    lax.fori_loop(1, ranks, out_sent, 0)
    lax.fori_loop(1, ranks, out_wait, 0)


def local(contexts, ranks, queries, key_value_rows, positions):
    heads = queries.shape[1] // HEAD
    group = SLICE // ranks
    ring = contexts // 4
    wide = min(4, ranks)
    deep = ranks // wide
    rows = heads * BLOCK
    block_rows = min(256, rows // 4)
    dma = pltpu.SemaphoreType.DMA
    return pl.pallas_call(
        functools.partial(kernel, contexts, ranks, heads, block_rows),
        out_shape=jax.ShapeDtypeStruct((group, ranks * heads * HEAD), BF16),
        in_specs=[pl.BlockSpec(memory_space=pltpu.HBM)] * 4,
        out_specs=pl.BlockSpec(memory_space=pltpu.HBM),
        scratch_shapes=[
            pltpu.VMEM((SLICE, heads * HEAD), BF16),
            pltpu.VMEM((2, group, ranks // 2 * HEAD), BF16),
            pltpu.VMEM((2, BLOCK), jnp.int32),
            pltpu.VMEM((8, HEAD), F32),
            pltpu.VMEM((2, ranks, 2, group, HEAD), BF16),
            pltpu.VMEM((2, 16, HEAD), BF16),
            pltpu.VMEM((contexts, SLOT, HEAD), BF16),
            pltpu.VMEM((wide // 2, deep, 2, group, HEAD), BF16),
            pltpu.VMEM((wide, deep, 2, group, HEAD), BF16),
            pltpu.VMEM((2, rows + 16, 2 * HEAD), BF16),
            pltpu.VMEM((HEAD, 4 * BLOCK), BF16),
            pltpu.VMEM((2 * HEAD, 4 * BLOCK), BF16),
            pltpu.VMEM((4 * BLOCK, 2 * HEAD), BF16),
            pltpu.VMEM((4 * BLOCK, 2 * HEAD), BF16),
            pltpu.VMEM((4 * BLOCK, 2 * HEAD), BF16),
            pltpu.VMEM((8, 8, HEAD), F32),
            pltpu.VMEM((2, rows, 2 * HEAD), F32),
            pltpu.VMEM((2, rows, 2 * HEAD), F32),
            pltpu.VMEM((2, rows, HEAD), F32),
            pltpu.VMEM((2, rows, HEAD), F32),
            pltpu.VMEM((rows, 2 * HEAD), BF16),
            pltpu.VMEM((rows, 2 * HEAD), BF16),
            pltpu.VMEM((BLOCK, HEAD), F32),
            pltpu.VMEM((BLOCK, HEAD), F32),
            pltpu.VMEM((SLICE, heads * HEAD), BF16),
            dma((4,)),
            dma((wide,)),
            dma((wide,)),
            dma((2, deep)),
            dma((2, deep)),
            dma((1,)),
            dma((1,)),
            dma((ring // 2 + 1, 8)),
            dma((ring // 2 + 1, 8)),
            dma((1,)),
            dma((1,)),
            dma((3,)),
            dma((3,)),
            dma((ranks, 2)),
            dma((ranks, 2)),
            dma((2,)),
        ],
        compiler_params=pltpu.CompilerParams(
            collective_id=0, has_side_effects=True, vmem_limit_bytes=60 * 1024 * 1024
        ),
        cost_estimate=pl.CostEstimate(
            flops=8 * rows * SLICE * contexts * HEAD // 2,
            bytes_accessed=4 * 1024 * 1024,
            transcendentals=rows * SLICE * contexts,
        ),
    )(queries, key_value_rows, positions.reshape(2, BLOCK), jnp.asarray(frequencies(HEAD)))


def solution(mesh):
    placed = (P("context", "tensor"), P(None, ("context", "tensor"), None), P("context"))
    return jax.shard_map(
        functools.partial(local, mesh.shape["context"], mesh.shape["tensor"]),
        mesh=mesh,
        in_specs=placed,
        out_specs=P(("context", "tensor"), None),
        check_vma=False,
    )
```

time: 74.8 us -> 68.8 us (0.920)
  Pallas kernels: 69.3 us -> 66.1 us
  local copies, waits for them, and re-layouts: 4.04 us -> 1.87 us
    pallas_call x1, Pallas kernels: 69.3 us -> 66.1 us  [local(): pl.pallas_call(functools.partial(kernel, contexts, ranks, heads, block_ro...]
    unnamed x9 -> x1, local copies, waits for them, and re-layouts: 4.04 us -> 1.87 us
where the time goes in v2:
time: 68.8 us; the launch traced here: 68 us
  Pallas kernels  66.1 us (96%)
  local copies, waits for them, and re-layouts  1.87 us (3%)
    pallas_call x1, Pallas kernels, local(): pl.pallas_call(functools.partial(kernel, contexts, ranks, heads, block_ro...  66.1 us
    unnamed x1, local copies, waits for them, and re-layouts  1.87 us

profile of v2, /device:TPU:6, one launch (start us, length us, event | category | flops | bytes accessed | tf_op | source)
XLA Modules:
  0.0 68.0 jit_solution(3138020201041151122)
XLA Ops:
  0.0 66.1 %shard_map.46 = bf16[16,16384]{1,0:T(8,128)(2,1)} custom-call(bf16[256,1024]{1,0:T(8,128)(2,1)} %q_hbm.1, bf16[2,16,1024]{2,1,0:T(8,128)(2,1)} %kv_hbm.1, s32[2,128]{1,0:T(2,128)} %bitcast.1, f32[8,128]{1,0:T(8,128)} %constant.2.clone.freq_hbm), custom_call_target="tpu_custom_call" | custom-call | flops 4294967296 | bytes 4194304 | tf_op jit(solution)/shard_map/pallas_call | solution.py:570
  66.1 1.9 %copy.6 = bf16[16,16384]{1,0:T(8,128)(2,1)} copy(bf16[16,16384]{1,0:T(8,128)(2,1)} %shard_map.46) | data formatting | bytes 1048576

commit v3 on v2

--- a/solution.py
+++ b/solution.py
@@ -352,26 +352,31 @@
             vals_small[span, 0:HEAD] = v_small * low
             vals_small[span, HEAD:2 * HEAD] = ones * low
 
-    def advance(n, owner, s):
-        starts = range(s * half_rows, (s + 1) * half_rows, block_rows)
+    def advance(n, owner, own_slice, after_block):
         keys = slice(0, n * BLOCK)
+        wide_piece = 2 * BLOCK
+        pieces = range(n // 2)
         bias_big = [bias[2 * i][0:1, :] for i in range(n)]
         bias_small = [bias[2 * i + 1][0:1, :] for i in range(n)]
-        scores = []
-        for start in starts:
+        starts = list(range(0, total, block_rows))
+
+        def split(products):
+            return [p[:, i * BLOCK:(i + 1) * BLOCK] for p in products for i in range(2)]
+
+        def score_piece(start, p):
             q = qq[owner, start:start + block_rows, :]
-            scores.append((
-                dot_nn(q[:, HEAD:2 * HEAD], keys_one[:, keys]), dot_nn(q, keys_two[:, keys])
-            ))
-        for start, (one, two) in zip(starts, scores):
+            span = slice(p * wide_piece, (p + 1) * wide_piece)
+            return dot_nn(q[:, HEAD:2 * HEAD], keys_one[:, span]), dot_nn(q, keys_two[:, span])
+
+        def maxima(start, scores):
             rows = slice(start, start + block_rows)
-            ones_of = [one[:, i * BLOCK:(i + 1) * BLOCK] for i in range(n)]
-            twos_of = [two[:, i * BLOCK:(i + 1) * BLOCK] for i in range(n)]
+            ones_of = split([one for one, two in scores])
+            twos_of = split([two for one, two in scores])
             big = functools.reduce(
-                jnp.maximum, ones_of + [x + w for x, w in zip(twos_of, bias_big)]
+                jnp.maximum, ones_of + [v + w for v, w in zip(twos_of, bias_big)]
             )
             small = functools.reduce(
-                jnp.maximum, [x + w for x, w in zip(twos_of, bias_small)]
+                jnp.maximum, [v + w for v, w in zip(twos_of, bias_small)]
             )
             old_big = max_big[owner, rows, :]
             old_small = max_small[owner, rows, :]
@@ -381,20 +386,43 @@
             max_small[owner, rows, :] = new_small
             alpha_big = jnp.exp2((old_big - new_big) * scale)
             alpha_small = jnp.exp2((old_small - new_small) * scale)
-            weights = [jnp.exp2((x - new_big) * scale).astype(BF16) for x in ones_of]
-            later = []
-            for x, wb, ws in zip(twos_of, bias_big, bias_small):
-                m = jnp.where(wb == 0.0, new_big, jnp.where(ws == 0.0, new_small, POSITIVE))
-                later.append(jnp.exp2((x - m) * scale).astype(BF16))
-            later = jnp.concatenate(later, axis=1)
-            every = jnp.concatenate(weights + [later], axis=1)
+            return ones_of, twos_of, new_big, new_small, alpha_big, alpha_small
+
+        def weigh(state, p):
+            ones_of, twos_of, new_big, new_small, alpha_big, alpha_small = state
+            first, second = [], []
+            for i in (2 * p, 2 * p + 1):
+                first.append(jnp.exp2((ones_of[i] - new_big) * scale).astype(BF16))
+                m = new_small
+                if own_slice:
+                    m = jnp.where(bias_small[i] == 0.0, new_small, POSITIVE)
+                m = jnp.where(bias_big[i] == 0.0, new_big, m)
+                second.append(jnp.exp2((twos_of[i] - m) * scale).astype(BF16))
+            return first, second
+
+        state = maxima(starts[0], [score_piece(starts[0], p) for p in pieces])
+        for b, start in enumerate(starts):
+            rows = slice(start, start + block_rows)
+            following_scores, first, second = [], [], []
+            for p in pieces:
+                if b + 1 < len(starts):
+                    following_scores.append(score_piece(starts[b + 1], p))
+                one, two = weigh(state, p)
+                first += one
+                second += two
+            later = jnp.concatenate(second, axis=1)
+            every = jnp.concatenate(first + second, axis=1)
             values = jnp.concatenate([vals_one[keys, :], vals_two[keys, :]], axis=0)
+            add_big = dot_nn(every, values)
+            add_small = dot_nn(later, vals_small[keys, :])
+            alpha_big, alpha_small = state[4], state[5]
+            if b + 1 < len(starts):
+                state = maxima(starts[b + 1], following_scores)
             wide_big = jnp.concatenate([alpha_big, alpha_big], axis=1)
             wide_small = jnp.concatenate([alpha_small, alpha_small], axis=1)
-            out_big[owner, rows, :] = out_big[owner, rows, :] * wide_big + dot_nn(every, values)
-            out_small[owner, rows, :] = (
-                out_small[owner, rows, :] * wide_small + dot_nn(later, vals_small[keys, :])
-            )
+            out_big[owner, rows, :] = out_big[owner, rows, :] * wide_big + add_big
+            out_small[owner, rows, :] = out_small[owner, rows, :] * wide_small + add_small
+            after_block(b)
 
     half_heads = heads // 2
     half_rows = total // 2
@@ -482,41 +510,58 @@
         lax.fori_loop(1, ranks, out_start, 0)
         out_keep(s).start()
 
-    def attend(k, ways, owner):
-        prepare([slot(k, way, s) for way in ways for s in range(2)], owner)
-        for s in range(2):
-            advance(2 * len(ways), owner, s)
-            arrive(k + 1, owner, s)
-
+    middle = total // block_rows // 2 - 1
+    final = total // block_rows - 1
     swap.wait_recv()
 
     def first_step(owner, carry):
-        attend(0, (0,), owner)
+        prepare([slot(0, 0, s) for s in range(2)], owner)
+        advance(2, owner, True, lambda b: None)
         return carry
 
     lax.fori_loop(0, 2, first_step, 0)
+    for s in range(2):
+        for layer in range(2):
+            arrive(1, s, layer)
 
     def step(i, carry):
-        attend(lax.div(i, 2) + 1, (0, 1), lax.rem(i, 2))
+        k = lax.div(i, 2) + 1
+        owner = lax.rem(i, 2)
+        prepare([slot(k, way, s) for way in range(2) for s in range(2)], owner)
+
+        def after_block(b):
+            if b == middle:
+                arrive(k + 1, owner, 0)
+            if b == final:
+                arrive(k + 1, owner, 1)
+
+        advance(4, owner, False, after_block)
         return carry
 
     if half_ring > 1:
         lax.fori_loop(0, 2 * (half_ring - 1), step, 0)
 
+    def return_block(b):
+        if b == middle:
+            give_back(0)
+        if b == final:
+            give_back(1)
+            part_copy(2).start()
+
+    def merge_block(b):
+        if b == middle:
+            part_copy(2).wait_recv()
+            part_copy(0).wait_recv()
+            finish(0)
+        if b == final:
+            part_copy(1).wait_recv()
+            finish(1)
+
     last = [slot(half_ring, 0, s) for s in range(2)]
     prepare(last, 0)
-    for s in range(2):
-        advance(2, 0, s)
-        give_back(s)
-    part_copy(2).start()
+    advance(2, 0, False, return_block)
     prepare(last, 1)
-    advance(2, 1, 0)
-    part_copy(2).wait_recv()
-    part_copy(0).wait_recv()
-    finish(0)
-    advance(2, 1, 1)
-    part_copy(1).wait_recv()
-    finish(1)
+    advance(2, 1, False, merge_block)
 
     def ring_sent(k, carry):
         for way in range(2):

time: 68.8 us -> 69.6 us (1.012)
  Pallas kernels: 66.1 us -> 67.3 us
    pallas_call x1, Pallas kernels: 66.1 us -> 67.3 us  [local(): pl.pallas_call(functools.partial(kernel, contexts, ranks, heads, block_ro...]
where the time goes in v3:
time: 69.6 us; the launch traced here: 69.1 us
  Pallas kernels  67.3 us (97%)
  local copies, waits for them, and re-layouts  1.87 us (3%)
    pallas_call x1, Pallas kernels, local(): pl.pallas_call(functools.partial(kernel, contexts, ranks, heads, block_ro...  67.3 us
    unnamed x1, local copies, waits for them, and re-layouts  1.87 us

profile of v3, /device:TPU:6, one launch (start us, length us, event | category | flops | bytes accessed | tf_op | source)
XLA Modules:
  0.0 69.1 jit_solution(12920818167448508558)
XLA Ops:
  0.0 67.3 %shard_map.46 = bf16[16,16384]{1,0:T(8,128)(2,1)} custom-call(bf16[256,1024]{1,0:T(8,128)(2,1)} %q_hbm.1, bf16[2,16,1024]{2,1,0:T(8,128)(2,1)} %kv_hbm.1, s32[2,128]{1,0:T(2,128)} %bitcast.1, f32[8,128]{1,0:T(8,128)} %constant.2.clone.freq_hbm), custom_call_target="tpu_custom_call" | custom-call | flops 4294967296 | bytes 4194304 | tf_op jit(solution)/shard_map/pallas_call | solution.py:615
  67.3 1.9 %copy.6 = bf16[16,16384]{1,0:T(8,128)(2,1)} copy(bf16[16,16384]{1,0:T(8,128)(2,1)} %shard_map.46) | data formatting | bytes 1048576

commit v4 on v2

--- a/solution.py
+++ b/solution.py
@@ -322,20 +322,21 @@
 
     lax.fori_loop(0, heads, diagonal, 0)
     for i in range(4):
-        vals_one[i * BLOCK:(i + 1) * BLOCK, HEAD:2 * HEAD] = ones
+        for bank in range(4):
+            vals_one[bank, i * BLOCK:(i + 1) * BLOCK, HEAD:2 * HEAD] = ones
 
     def flag(condition):
         return jnp.where(condition, 1.0, 0.0)
 
-    def prepare(places, owner):
+    def prepare(places, owner, bank):
         asker = qq[owner, total:total + 16, 0:HEAD].astype(F32)[0:1, :]
         my_small = jnp.minimum(asker, blocks - 1 - asker)
         for i, where in enumerate(places):
             small = slab[where, NUMBER:NUMBER + 16].astype(F32)[0:1, :]
             low = flag(small < my_small)
             high = flag(small > my_small)
-            bias[2 * i] = jnp.broadcast_to((high - 1.0) * POSITIVE, (8, HEAD))
-            bias[2 * i + 1] = jnp.broadcast_to((low - 1.0) * POSITIVE, (8, HEAD))
+            bias[bank, 2 * i] = jnp.broadcast_to((high - 1.0) * POSITIVE, (8, HEAD))
+            bias[bank, 2 * i + 1] = jnp.broadcast_to((low - 1.0) * POSITIVE, (8, HEAD))
             low = low.astype(BF16)
             high = high.astype(BF16)
             span = slice(i * BLOCK, (i + 1) * BLOCK)
@@ -343,25 +344,25 @@
             k_big = slab[where, BIG:BIG + BLOCK]
             v_small = slab[where, BLOCK:2 * BLOCK]
             v_big = slab[where, BIG + BLOCK:SLOT]
-            keys_one[:, span] = k_small
-            keys_two[0:HEAD, span] = k_small * low
-            keys_two[HEAD:2 * HEAD, span] = k_big * high
-            vals_one[span, 0:HEAD] = v_small
-            vals_two[span, 0:HEAD] = v_big * high
-            vals_two[span, HEAD:2 * HEAD] = ones * high
-            vals_small[span, 0:HEAD] = v_small * low
-            vals_small[span, HEAD:2 * HEAD] = ones * low
-
-    def advance(n, owner, s):
+            keys_one[bank, :, span] = k_small
+            keys_two[bank, 0:HEAD, span] = k_small * low
+            keys_two[bank, HEAD:2 * HEAD, span] = k_big * high
+            vals_one[bank, span, 0:HEAD] = v_small
+            vals_two[bank, span, 0:HEAD] = v_big * high
+            vals_two[bank, span, HEAD:2 * HEAD] = ones * high
+            vals_small[bank, span, 0:HEAD] = v_small * low
+            vals_small[bank, span, HEAD:2 * HEAD] = ones * low
+
+    def advance(n, owner, s, bank, own_slice=False):
         starts = range(s * half_rows, (s + 1) * half_rows, block_rows)
         keys = slice(0, n * BLOCK)
-        bias_big = [bias[2 * i][0:1, :] for i in range(n)]
-        bias_small = [bias[2 * i + 1][0:1, :] for i in range(n)]
+        bias_big = [bias[bank, 2 * i][0:1, :] for i in range(n)]
+        bias_small = [bias[bank, 2 * i + 1][0:1, :] for i in range(n)]
         scores = []
         for start in starts:
             q = qq[owner, start:start + block_rows, :]
             scores.append((
-                dot_nn(q[:, HEAD:2 * HEAD], keys_one[:, keys]), dot_nn(q, keys_two[:, keys])
+                dot_nn(q[:, HEAD:2 * HEAD], keys_one[bank, :, keys]), dot_nn(q, keys_two[bank, :, keys])
             ))
         for start, (one, two) in zip(starts, scores):
             rows = slice(start, start + block_rows)
@@ -384,16 +385,19 @@
             weights = [jnp.exp2((x - new_big) * scale).astype(BF16) for x in ones_of]
             later = []
             for x, wb, ws in zip(twos_of, bias_big, bias_small):
-                m = jnp.where(wb == 0.0, new_big, jnp.where(ws == 0.0, new_small, POSITIVE))
+                m = new_small
+                if own_slice:
+                    m = jnp.where(ws == 0.0, m, POSITIVE)
+                m = jnp.where(wb == 0.0, new_big, m)
                 later.append(jnp.exp2((x - m) * scale).astype(BF16))
             later = jnp.concatenate(later, axis=1)
             every = jnp.concatenate(weights + [later], axis=1)
-            values = jnp.concatenate([vals_one[keys, :], vals_two[keys, :]], axis=0)
+            values = jnp.concatenate([vals_one[bank, keys, :], vals_two[bank, keys, :]], axis=0)
             wide_big = jnp.concatenate([alpha_big, alpha_big], axis=1)
             wide_small = jnp.concatenate([alpha_small, alpha_small], axis=1)
             out_big[owner, rows, :] = out_big[owner, rows, :] * wide_big + dot_nn(every, values)
             out_small[owner, rows, :] = (
-                out_small[owner, rows, :] * wide_small + dot_nn(later, vals_small[keys, :])
+                out_small[owner, rows, :] * wide_small + dot_nn(later, vals_small[bank, keys, :])
             )
 
     half_heads = heads // 2
@@ -406,8 +410,8 @@
         return best * scale + jnp.log(weight) * log2_e
 
     def part_copy(i):
-        if i == 2:
-            src, dst = sums_out, sums_in
+        if i >= 2:
+            src, dst = sums_out.at[i - 2], sums_in.at[i - 2]
         else:
             src = part_out.at[pl.ds(i * half_rows, half_rows)]
             dst = part_in.at[pl.ds(i * half_rows, half_rows)]
@@ -417,7 +421,7 @@
         )
 
     def give_back(s):
-        packed = jnp.zeros((BLOCK, HEAD), F32) if s == 0 else sums_out[...]
+        packed = jnp.zeros((BLOCK, HEAD), F32)
         for h in range(s * half_heads, (s + 1) * half_heads):
             rows = slice(h * BLOCK, (h + 1) * BLOCK)
             for i, (best, sums) in enumerate(((max_small, out_small), (max_big, out_big))):
@@ -428,8 +432,9 @@
                 first = h * 16 + i * 8
                 inside = jnp.logical_and(lane >= first, lane < first + 8)
                 packed = jnp.where(inside, log_sum(best[0, rows, :], weight), packed)
-        sums_out[...] = packed
+        sums_out[s] = packed
         part_copy(s).start()
+        part_copy(2 + s).start()
 
     width = half_heads * HEAD
 
@@ -463,7 +468,7 @@
                 weight = sums[1, rows, HEAD:2 * HEAD]
                 mine = log_sum(best[1, rows, :], weight)
                 first = h * 16 + i * 8
-                theirs = jnp.broadcast_to(sums_in[:, first:first + 1], (BLOCK, HEAD))
+                theirs = jnp.broadcast_to(sums_in[s, :, first:first + 1], (BLOCK, HEAD))
                 top = jnp.maximum(mine, theirs)
                 mine = jnp.exp2(mine - top)
                 theirs = jnp.exp2(theirs - top)
@@ -482,40 +487,56 @@
         lax.fori_loop(1, ranks, out_start, 0)
         out_keep(s).start()
 
-    def attend(k, ways, owner):
-        prepare([slot(k, way, s) for way in ways for s in range(2)], owner)
+    def near_places(k):
+        return [slot(k, way, s) for way in range(2) for s in range(2)]
+
+    swap.wait_recv()
+
+    def first_step(owner, carry):
+        prepare([slot(0, 0, s) for s in range(2)], owner, 0)
         for s in range(2):
-            advance(2 * len(ways), owner, s)
+            advance(2, owner, s, 0, True)
+        return carry
+
+    lax.fori_loop(0, 2, first_step, 0)
+    for s in range(2):
+        for layer in range(2):
+            arrive(1, s, layer)
+
+    def step(i, carry):
+        k = lax.div(i, 2) + 1
+        owner = lax.rem(i, 2)
+        prepare(near_places(k), owner, 0)
+        for s in range(2):
+            advance(4, owner, s, 0)
             arrive(k + 1, owner, s)
-
-    swap.wait_recv()
-
-    def first_step(owner, carry):
-        attend(0, (0,), owner)
-        return carry
-
-    lax.fori_loop(0, 2, first_step, 0)
-
-    def step(i, carry):
-        attend(lax.div(i, 2) + 1, (0, 1), lax.rem(i, 2))
-        return carry
-
-    if half_ring > 1:
-        lax.fori_loop(0, 2 * (half_ring - 1), step, 0)
-
+        return carry
+
+    if half_ring > 2:
+        lax.fori_loop(0, 2 * (half_ring - 2), step, 0)
+
+    places = near_places(half_ring - 1)
     last = [slot(half_ring, 0, s) for s in range(2)]
-    prepare(last, 0)
-    for s in range(2):
-        advance(2, 0, s)
-        give_back(s)
-    part_copy(2).start()
-    prepare(last, 1)
-    advance(2, 1, 0)
+    for owner in range(2):
+        prepare(places, owner, owner)
+        advance(4, owner, 0, owner)
+        for layer in range(2):
+            arrive(half_ring, owner, layer)
+    prepare(last, 0, 2)
+    advance(2, 0, 0, 2)
+    give_back(0)
+    prepare(last, 1, 3)
+    advance(2, 1, 0, 3)
+    advance(4, 0, 1, 0)
+    part_copy(0).wait_recv()
     part_copy(2).wait_recv()
-    part_copy(0).wait_recv()
     finish(0)
-    advance(2, 1, 1)
+    advance(2, 0, 1, 2)
+    give_back(1)
+    advance(4, 1, 1, 1)
+    advance(2, 1, 1, 3)
     part_copy(1).wait_recv()
+    part_copy(3).wait_recv()
     finish(1)
 
     def ring_sent(k, carry):
@@ -550,7 +571,7 @@
     id_copy(z).wait_send()
     lax.fori_loop(0, half_ring, ring_sent, 0)
     swap.wait_send()
-    for i in range(3):
+    for i in range(4):
         part_copy(i).wait_send()
     for s in range(2):
         out_keep(s).wait()
@@ -583,20 +604,20 @@
             pltpu.VMEM((wide // 2, deep, 2, group, HEAD), BF16),
             pltpu.VMEM((wide, deep, 2, group, HEAD), BF16),
             pltpu.VMEM((2, rows + 16, 2 * HEAD), BF16),
-            pltpu.VMEM((HEAD, 4 * BLOCK), BF16),
-            pltpu.VMEM((2 * HEAD, 4 * BLOCK), BF16),
-            pltpu.VMEM((4 * BLOCK, 2 * HEAD), BF16),
-            pltpu.VMEM((4 * BLOCK, 2 * HEAD), BF16),
-            pltpu.VMEM((4 * BLOCK, 2 * HEAD), BF16),
-            pltpu.VMEM((8, 8, HEAD), F32),
+            pltpu.VMEM((4, HEAD, 4 * BLOCK), BF16),
+            pltpu.VMEM((4, 2 * HEAD, 4 * BLOCK), BF16),
+            pltpu.VMEM((4, 4 * BLOCK, 2 * HEAD), BF16),
+            pltpu.VMEM((4, 4 * BLOCK, 2 * HEAD), BF16),
+            pltpu.VMEM((4, 4 * BLOCK, 2 * HEAD), BF16),
+            pltpu.VMEM((4, 8, 8, HEAD), F32),
             pltpu.VMEM((2, rows, 2 * HEAD), F32),
             pltpu.VMEM((2, rows, 2 * HEAD), F32),
             pltpu.VMEM((2, rows, HEAD), F32),
             pltpu.VMEM((2, rows, HEAD), F32),
             pltpu.VMEM((rows, 2 * HEAD), BF16),
             pltpu.VMEM((rows, 2 * HEAD), BF16),
-            pltpu.VMEM((BLOCK, HEAD), F32),
-            pltpu.VMEM((BLOCK, HEAD), F32),
+            pltpu.VMEM((2, BLOCK, HEAD), F32),
+            pltpu.VMEM((2, BLOCK, HEAD), F32),
             pltpu.VMEM((SLICE, heads * HEAD), BF16),
             dma((4,)),
             dma((wide,)),
@@ -609,8 +630,8 @@
             dma((ring // 2 + 1, 8)),
             dma((1,)),
             dma((1,)),
-            dma((3,)),
-            dma((3,)),
+            dma((4,)),
+            dma((4,)),
             dma((ranks, 2)),
             dma((ranks, 2)),
             dma((2,)),

time: 68.8 us -> 68 us (0.988)
  Pallas kernels: 66.1 us -> 65 us
    pallas_call x1, Pallas kernels: 66.1 us -> 65 us  [local(): pl.pallas_call(functools.partial(kernel, contexts, ranks, heads, block_ro...]
where the time goes in v4:
time: 68 us; the launch traced here: 66.9 us
  Pallas kernels  65 us (96%)
  local copies, waits for them, and re-layouts  1.87 us (3%)
    pallas_call x1, Pallas kernels, local(): pl.pallas_call(functools.partial(kernel, contexts, ranks, heads, block_ro...  65 us
    unnamed x1, local copies, waits for them, and re-layouts  1.87 us

profile of v4, /device:TPU:6, one launch (start us, length us, event | category | flops | bytes accessed | tf_op | source)
XLA Modules:
  0.0 66.9 jit_solution(9019828889350480300)
XLA Ops:
  0.0 65.0 %shard_map.46 = bf16[16,16384]{1,0:T(8,128)(2,1)} custom-call(bf16[256,1024]{1,0:T(8,128)(2,1)} %q_hbm.1, bf16[2,16,1024]{2,1,0:T(8,128)(2,1)} %kv_hbm.1, s32[2,128]{1,0:T(2,128)} %bitcast.1, f32[8,128]{1,0:T(8,128)} %constant.2.clone.freq_hbm), custom_call_target="tpu_custom_call" | custom-call | flops 4294967296 | bytes 4194304 | tf_op jit(solution)/shard_map/pallas_call | solution.py:591
  65.0 1.9 %copy.6 = bf16[16,16384]{1,0:T(8,128)(2,1)} copy(bf16[16,16384]{1,0:T(8,128)(2,1)} %shard_map.46) | data formatting | bytes 1048576

commit v5 on v4

--- a/solution.py
+++ b/solution.py
@@ -19,10 +19,10 @@
 BF16 = jnp.bfloat16
 
 
-LAYERS = ((0, 2 * BLOCK + 16), (2 * BLOCK + 16, 2 * BLOCK))
 NUMBER = 2 * BLOCK
 BIG = 2 * BLOCK + 16
 SLOT = 4 * BLOCK + 16
+LAYER = SLOT // 3
 
 
 def frequencies(width):
@@ -44,7 +44,7 @@
     queries, kv_ref, place_ref, freq_ref, landed, numbers, slab, staged, crossed,
     qq, keys_one, keys_two, vals_one, vals_two, vals_small, bias,
     out_big, out_small, max_big, max_small, part_out, part_in, sums_out, sums_in, done,
-    in_sem, x_send, x_recv, z_send, z_recv, m_send, m_recv, r_send, r_recv, g_send, g_recv, p_send, p_recv, o_send, o_recv, k_sem,
+    in_sem, x_send, x_recv, z_send, z_recv, m_send, m_recv, r_send, r_recv, w_send, w_recv, g_send, g_recv, p_send, p_recv, o_send, o_recv, k_sem,
 ):
     ring = contexts // 4
     group = SLICE // ranks
@@ -74,6 +74,8 @@
     across = at(1 - z, y, core)
     x = lax.rem(t, wide)
     low_z = lax.div(t, wide)
+    odd = lax.rem(x, 2)
+    twin = t + 1 - 2 * odd
 
     def row_peer(k):
         return low_z * wide + lax.rem(x + k, wide)
@@ -202,43 +204,57 @@
     def slot(k, way, s):
         return at(lax.rem(z + s, 2), turn(y + ring - (1 - 2 * way) * k), core)
 
-    def move(where, layer, send, recv, target):
-        low, size = LAYERS[layer]
-        view = slab.at[where, pl.ds(low, size)]
+    def view(k, way, s, layer):
+        start = pl.multiple_of(layer * LAYER, 16)
+        return slab.at[slot(k, way, s), pl.ds(start, LAYER)]
+
+    own = 1 + odd
+
+    def ring_move(k, way, s, part, arrived):
+        here = view(k, way, s, part * own)
+        e = 4 * way + 2 * s + part
         return pltpu.make_async_remote_copy(
-            src_ref=view, dst_ref=view, send_sem=send, recv_sem=recv,
-            device_id=(target, t), device_id_type=MESH,
-        )
-
-    def entry(way, s, layer):
-        return 4 * way + 2 * s + layer
-
-    def ring_copy(k, way, s, layer):
-        e = entry(way, s, layer)
-        target = at(z, turn(y + ring + 1 - 2 * way), core)
-        return move(
-            slot(k, way, s), layer, r_send.at[k, e], r_recv.at[k + 1, e], target
-        )
-
-    def ring_wait(k, way, s, layer):
-        e = entry(way, s, layer)
-        move(
-            slot(k, way, s), layer, r_send.at[k, e], r_recv.at[k, e], after
-        ).wait_recv()
+            src_ref=here, dst_ref=here, send_sem=r_send.at[k, e], recv_sem=r_recv.at[arrived, e],
+            device_id=(at(z, turn(y + ring + 1 - 2 * way), core), t), device_id_type=MESH,
+        )
+
+    def ring_copy(k, way, s, part):
+        return ring_move(k, way, s, part, k + 1)
+
+    def ring_wait(k, way, s, part):
+        ring_move(k, way, s, part, k).wait_recv()
+
+    def twin_move(k, way, s, layer):
+        here = view(k, way, s, layer)
+        e = 2 * way + s
+        return pltpu.make_async_remote_copy(
+            src_ref=here, dst_ref=here, send_sem=w_send.at[k, e], recv_sem=w_recv.at[k, e],
+            device_id=(c, twin), device_id_type=MESH,
+        )
 
     def goes_on(k, way, s):
         return jnp.logical_or(k < half_ring - 1, jnp.logical_and(k == half_ring - 1, s == way))
 
-    def arrive(k, s, layer):
+    def arrive(k, s, part):
         for way in range(2):
 
             @pl.when(goes_on(k - 1, way, s))
             def _():
-                ring_wait(k, way, s, layer)
+                ring_wait(k, way, s, part)
 
                 @pl.when(goes_on(k, way, s))
                 def _():
-                    ring_copy(k, way, s, layer).start()
+                    ring_copy(k, way, s, part).start()
+
+                if part == 1:
+                    twin_move(k, way, s, own).start()
+
+    def arrive_twin(k, s):
+        for way in range(2):
+
+            @pl.when(goes_on(k - 1, way, s))
+            def _():
+                twin_move(k, way, s, 3 - own).wait_recv()
 
     def arrange(zz):
         where = at(zz, y, core)
@@ -262,10 +278,10 @@
         slab[where, BIG + BLOCK:SLOT] = halves[3].astype(BF16)
 
     def launch(s):
-        for layer in range(2):
+        for part in range(2):
             for way in range(2):
                 if half_ring > 1 or s == way:
-                    ring_copy(0, way, s, layer).start()
+                    ring_copy(0, way, s, part).start()
 
     first_id = number(0)
     first_small = first_id < blocks / 2
@@ -487,54 +503,61 @@
         lax.fori_loop(1, ranks, out_start, 0)
         out_keep(s).start()
 
-    def near_places(k):
+    def places(k):
+        if k == 0 or k == half_ring:
+            return [slot(k, 0, s) for s in range(2)]
         return [slot(k, way, s) for way in range(2) for s in range(2)]
 
+    def take(k, s):
+        for part in range(2):
+            arrive(k, s, part)
+
+    def take_twin(k):
+        for s in range(2):
+            arrive_twin(k, s)
+
+    def compute(k, s):
+        here = places(k)
+
+        def both(owner, carry):
+            bank = 2 * (k % 2) + owner
+            if s == 0:
+                prepare(here, owner, bank)
+            advance(len(here), owner, s, bank, k == 0)
+            return carry
+
+        lax.fori_loop(0, 2, both, 0)
+
     swap.wait_recv()
-
-    def first_step(owner, carry):
-        prepare([slot(0, 0, s) for s in range(2)], owner, 0)
-        for s in range(2):
-            advance(2, owner, s, 0, True)
-        return carry
-
-    lax.fori_loop(0, 2, first_step, 0)
-    for s in range(2):
-        for layer in range(2):
-            arrive(1, s, layer)
-
-    def step(i, carry):
-        k = lax.div(i, 2) + 1
-        owner = lax.rem(i, 2)
-        prepare(near_places(k), owner, 0)
-        for s in range(2):
-            advance(4, owner, s, 0)
-            arrive(k + 1, owner, s)
-        return carry
-
-    if half_ring > 2:
-        lax.fori_loop(0, 2 * (half_ring - 2), step, 0)
-
-    places = near_places(half_ring - 1)
-    last = [slot(half_ring, 0, s) for s in range(2)]
+    compute(0, 0)
+    take(1, 0)
+    take(1, 1)
+    compute(0, 1)
+    for k in range(1, half_ring):
+        take(k + 1, 0)
+        if k > 1:
+            compute(k - 1, 1)
+        take(k + 1, 1)
+        take_twin(k)
+        compute(k, 0)
+
+    near = 2 * ((half_ring - 1) % 2)
+    final = 2 - near
+    last = places(half_ring)
+    advance(4, 0, 1, near)
+    take_twin(half_ring)
     for owner in range(2):
-        prepare(places, owner, owner)
-        advance(4, owner, 0, owner)
-        for layer in range(2):
-            arrive(half_ring, owner, layer)
-    prepare(last, 0, 2)
-    advance(2, 0, 0, 2)
+        prepare(last, owner, final + owner)
+    advance(2, 0, 0, final)
     give_back(0)
-    prepare(last, 1, 3)
-    advance(2, 1, 0, 3)
-    advance(4, 0, 1, 0)
+    advance(2, 1, 0, final + 1)
+    advance(2, 0, 1, final)
+    give_back(1)
     part_copy(0).wait_recv()
     part_copy(2).wait_recv()
     finish(0)
-    advance(2, 0, 1, 2)
-    give_back(1)
-    advance(4, 1, 1, 1)
-    advance(2, 1, 1, 3)
+    advance(4, 1, 1, near + 1)
+    advance(2, 1, 1, final + 1)
     part_copy(1).wait_recv()
     part_copy(3).wait_recv()
     finish(1)
@@ -542,11 +565,12 @@
     def ring_sent(k, carry):
         for way in range(2):
             for s in range(2):
-                for layer in range(2):
-
-                    @pl.when(goes_on(k, way, s))
-                    def _():
-                        ring_copy(k, way, s, layer).wait_send()
+
+                @pl.when(goes_on(k, way, s))
+                def _():
+                    for part in range(2):
+                        ring_copy(k, way, s, part).wait_send()
+                    twin_move(k + 1, way, s, own).wait_send()
 
         return carry
 
@@ -628,6 +652,8 @@
             dma((1,)),
             dma((ring // 2 + 1, 8)),
             dma((ring // 2 + 1, 8)),
+            dma((ring // 2 + 1, 4)),
+            dma((ring // 2 + 1, 4)),
             dma((1,)),
             dma((1,)),
             dma((4,)),

time: 68 us -> 68.9 us (1.013); the launches traced: 66.9 us -> 68.7 us
  Pallas kernels: 65 us -> 66.8 us
    pallas_call x1, Pallas kernels: 65 us -> 66.8 us  [local(): pl.pallas_call(functools.partial(kernel, contexts, ranks, heads, block_ro...]
where the time goes in v5:
time: 68.9 us; the launch traced here: 68.7 us
  Pallas kernels  66.8 us (97%)
  local copies, waits for them, and re-layouts  1.87 us (3%)
    pallas_call x1, Pallas kernels, local(): pl.pallas_call(functools.partial(kernel, contexts, ranks, heads, block_ro...  66.8 us
    unnamed x1, local copies, waits for them, and re-layouts  1.87 us

profile of v5, /device:TPU:6, one launch (start us, length us, event | category | flops | bytes accessed | tf_op | source)
XLA Modules:
  0.0 68.7 jit_solution(9270089839381898103)
XLA Ops:
  0.0 66.8 %shard_map.46 = bf16[16,16384]{1,0:T(8,128)(2,1)} custom-call(bf16[256,1024]{1,0:T(8,128)(2,1)} %q_hbm.1, bf16[2,16,1024]{2,1,0:T(8,128)(2,1)} %kv_hbm.1, s32[2,128]{1,0:T(2,128)} %bitcast.1, f32[8,128]{1,0:T(8,128)} %constant.2.clone.freq_hbm), custom_call_target="tpu_custom_call" | custom-call | flops 4294967296 | bytes 4194304 | tf_op jit(solution)/shard_map/pallas_call | solution.py:615
  66.8 1.9 %copy.6 = bf16[16,16384]{1,0:T(8,128)(2,1)} copy(bf16[16,16384]{1,0:T(8,128)(2,1)} %shard_map.46) | data formatting | bytes 1048576

commit v6 on v4

--- a/solution.py
+++ b/solution.py
@@ -586,7 +586,7 @@
     wide = min(4, ranks)
     deep = ranks // wide
     rows = heads * BLOCK
-    block_rows = min(256, rows // 4)
+    block_rows = min(512, rows // 2)
     dma = pltpu.SemaphoreType.DMA
     return pl.pallas_call(
         functools.partial(kernel, contexts, ranks, heads, block_rows),

time: 68 us -> 68.7 us (1.010)
  Pallas kernels: 65 us -> 65.8 us
    pallas_call x1, Pallas kernels: 65 us -> 65.8 us  [local(): pl.pallas_call(functools.partial(kernel, contexts, ranks, heads, block_ro...]
where the time goes in v6:
time: 68.7 us; the launch traced here: 67.7 us
  Pallas kernels  65.8 us (96%)
  local copies, waits for them, and re-layouts  1.87 us (3%)
    pallas_call x1, Pallas kernels, local(): pl.pallas_call(functools.partial(kernel, contexts, ranks, heads, block_ro...  65.8 us
    unnamed x1, local copies, waits for them, and re-layouts  1.87 us

profile of v6, /device:TPU:6, one launch (start us, length us, event | category | flops | bytes accessed | tf_op | source)
XLA Modules:
  0.0 67.7 jit_solution(12855833475876482421)
XLA Ops:
  0.0 65.8 %shard_map.46 = bf16[16,16384]{1,0:T(8,128)(2,1)} custom-call(bf16[256,1024]{1,0:T(8,128)(2,1)} %q_hbm.1, bf16[2,16,1024]{2,1,0:T(8,128)(2,1)} %kv_hbm.1, s32[2,128]{1,0:T(2,128)} %bitcast.1, f32[8,128]{1,0:T(8,128)} %constant.2.clone.freq_hbm), custom_call_target="tpu_custom_call" | custom-call | flops 4294967296 | bytes 4194304 | tf_op jit(solution)/shard_map/pallas_call | solution.py:591
  65.8 1.9 %copy.6 = bf16[16,16384]{1,0:T(8,128)(2,1)} copy(bf16[16,16384]{1,0:T(8,128)(2,1)} %shard_map.46) | data formatting | bytes 1048576

commit v7 on v4

--- a/solution.py
+++ b/solution.py
@@ -484,7 +484,9 @@
             out_move(pt, t, s, pt, t, pt).start()
             return carry
 
-        lax.fori_loop(1, ranks, out_start, 0)
+        edges = (1, max(ranks // 4, 1), max(ranks // 2, 1), ranks)
+        for low, high in ((edges[2], edges[3]), (edges[1], edges[2]), (edges[0], edges[1])):
+            lax.fori_loop(low, high, out_start, 0)
         out_keep(s).start()
 
     def near_places(k):

time: 68 us -> 68.6 us (level)
  the two profiles are of different devices: /device:TPU:6 before, /device:TPU:1 now
where the time goes in v7:
time: 68.6 us; the launch traced here: 68.5 us
  Pallas kernels  66.6 us (97%)
  local copies, waits for them, and re-layouts  1.87 us (3%)
    pallas_call x1, Pallas kernels, local(): pl.pallas_call(functools.partial(kernel, contexts, ranks, heads, block_ro...  66.6 us
    unnamed x1, local copies, waits for them, and re-layouts  1.87 us

profile of v7, /device:TPU:1, one launch (start us, length us, event | category | flops | bytes accessed | tf_op | source)
XLA Modules:
  0.0 68.5 jit_solution(16972782785007815850)
XLA Ops:
  0.0 66.6 %shard_map.46 = bf16[16,16384]{1,0:T(8,128)(2,1)} custom-call(bf16[256,1024]{1,0:T(8,128)(2,1)} %q_hbm.1, bf16[2,16,1024]{2,1,0:T(8,128)(2,1)} %kv_hbm.1, s32[2,128]{1,0:T(2,128)} %bitcast.1, f32[8,128]{1,0:T(8,128)} %constant.2.clone.freq_hbm), custom_call_target="tpu_custom_call" | custom-call | flops 4294967296 | bytes 4194304 | tf_op jit(solution)/shard_map/pallas_call | solution.py:593
  66.6 1.9 %copy.6 = bf16[16,16384]{1,0:T(8,128)(2,1)} copy(bf16[16,16384]{1,0:T(8,128)(2,1)} %shard_map.46) | data formatting | bytes 1048576
